TPU v7x, 512 devices: a whole 4x4x16 slice. The times are simulated.
512 devices in a mesh: col: 16 (over x_hi, y, core), fac: 32 (over x_lo, z).
Axes of the slice: x: 4 (x_hi: 2, x_lo: 2; x = x_hi * 2 + x_lo), y: 4, z: 16, core: 2. Of those that a mesh axis runs over, the one named last changes fastest.
Arguments:
- facets: bfloat16 [2, 4096, 4096], P(None, 'col', 'fac'), may hold values from -6 to 6
- row_taper: float32 [4096], P('col'), may hold values from 0.5 to 1.5
- column_taper: float32 [4096], replicated, may hold values from 0.5 to 1.5
- column_place: int32 [1], replicated, may hold values from 0 to 511
- row_offset: int32 [16], replicated, may hold values from 0 to 4095
- column_offset: int32 [32], replicated, may hold values from 0 to 4095
- slot_subgrid: int32 [16, 32], replicated, may hold values from 0 to 31, each once within a row
Outputs:
- subgrids: float32 [16, 32, 2, 512, 128], P('col', 'fac')
All inputs are finite; a program needn't handle non-finite values.
Results may differ from a plain program's by a relative error of at most 0.0052.
Values may be sent and summed in bfloat16 or wider, within the bound.
No kernel may reach another device: no remote copies, remote signals or barrier semaphores. Data moves between devices by JAX's collectives and lax.ppermute only.
A program may use at most 64 MiB of HBM per device.

v0:
```python
import math

import jax
import jax.numpy as jnp
import numpy as np
from jax import lax
from jax.experimental import pallas as pl
from jax.experimental.pallas import tpu as pltpu
from jax.sharding import Mesh, PartitionSpec as P

FACET = 4096
STRIP = 128
SUBGRID = 512
HALF = 256
SPLIT = ("xh", "y", "core", "xl", "zh", "zl")
SIZES = (2, 4, 2, 2, 4, 4)
COL = SPLIT[:3]
FAC = SPLIT[3:]
F32 = jnp.float32
BF16 = jnp.bfloat16
VMEM = pl.BlockSpec(memory_space=pltpu.VMEM)
SMEM = pl.BlockSpec(memory_space=pltpu.SMEM)
NT = (((1,), (1,)), ((), ()))


def base_table():
    k = np.arange(STRIP)[:, None]
    j = np.arange(HALF)[None, :]
    angle = (k * j % FACET) * (2.0 * math.pi / FACET)
    scale = 1.0 / math.sqrt(FACET)
    return np.stack([np.cos(angle) * scale, -np.sin(angle) * scale]).astype(np.float32)


def unit(phase):
    angle = phase.astype(F32) * (2.0 * math.pi / FACET)
    return jnp.cos(angle), -jnp.sin(angle)


def turned(base_ref, turned_ref, block):
    k = lax.broadcasted_iota(jnp.int32, (16, HALF), 0)
    real, imag = unit((k * block & 15) * HALF)
    for row in range(0, STRIP, 16):
        rows = pl.ds(row, 16)
        base_real, base_imag = base_ref[0, rows, :], base_ref[1, rows, :]
        turned_ref[0, rows, :] = base_real * real - base_imag * imag
        turned_ref[1, rows, :] = base_real * imag + base_imag * real


def fill_tables(starts, blocks, base_ref, out_ref, turned_ref):
    count = len(starts)
    padded = 8
    row = lax.broadcasted_iota(jnp.int32, (padded, HALF), 0)
    lane = lax.broadcasted_iota(jnp.int32, (padded, HALF), 1)
    first = jnp.zeros((padded, HALF), jnp.int32)
    for n, start in enumerate(starts):
        first = jnp.where(row == n, start, first)
    for c, block in enumerate(blocks):
        turned(base_ref, turned_ref, block)
        real, imag = unit(first * (block * HALF + lane) & (FACET - 1))
        for k in range(0, STRIP, 16):
            rows = pl.ds(k, 16)
            base_real, base_imag = turned_ref[0, rows, :], turned_ref[1, rows, :]
            for n in range(count):
                own_real, own_imag = real[n : n + 1], imag[n : n + 1]
                out_ref[n, rows, HALF * c : HALF * (c + 1)] = (
                    own_real * base_real - own_imag * base_imag
                ).astype(BF16)
                out_ref[n, pl.ds(STRIP + k, 16), HALF * c : HALF * (c + 1)] = (
                    own_real * base_imag + own_imag * base_real
                ).astype(BF16)


def prepare_kernel(facets_ref, row_ref, column_ref, out_ref):
    fac = (lax.axis_index("xl") * 4 + lax.axis_index("zh")) * 4 + lax.axis_index("zl")
    column = column_ref[pl.ds(fac, 1), :]
    for part in range(2):
        scaled = facets_ref[part].astype(F32) * column
        out_ref[STRIP * part : STRIP * (part + 1), :] = (scaled.T * row_ref[...]).astype(BF16)


def encode_kernel(row_offset_ref, base_ref, out_ref, turned_ref):
    core = lax.axis_index("core")
    pair = lax.axis_index("xh") * 4 + lax.axis_index("y")
    starts = [row_offset_ref[2 * n + core] for n in range(8)]
    fill_tables(starts, [2 * pair + core, 2 * pair + 1 - core], base_ref, out_ref, turned_ref)


def decode_kernel(slot_ref, offset_ref, base_ref, out_ref, turned_ref):
    column = (lax.axis_index("xh") * 4 + lax.axis_index("y")) * 2 + lax.axis_index("core")
    zh = lax.axis_index("zh")
    slot = lax.axis_index("xl") * 16 + lax.axis_index("zl")
    starts = [offset_ref[slot_ref[column, slot + 4 * n]] for n in range(4)]
    blocks = [2 * zh, 2 * zh + 1, 2 * zh + 8, 2 * zh + 9]
    fill_tables(starts, blocks, base_ref, out_ref, turned_ref)


def strip_kernel(own_ref, other_ref, table_ref, out_ref):
    for n in range(8):
        product = lax.dot_general(
            own_ref[...], table_ref[n, :, :HALF], NT, preferred_element_type=F32
        ) + lax.dot_general(
            other_ref[...], table_ref[n, :, HALF:], NT, preferred_element_type=F32
        )
        out_ref[n, :, :STRIP] = (product[:STRIP, :STRIP] - product[STRIP:, STRIP:]).astype(BF16)
        out_ref[n, :, STRIP:] = (product[:STRIP, STRIP:] + product[STRIP:, :STRIP]).astype(BF16)


def sum_kernel(parts_ref, out_ref):
    total = parts_ref[0].astype(F32)
    for n in range(1, 8):
        total += parts_ref[n].astype(F32)
    total = total.astype(BF16)
    for n in range(8):
        out_ref[n] = total


def subgrid_kernel(strip_ref, table_ref, out_ref):
    strip = strip_ref[...].reshape(8 * STRIP, 2 * STRIP)
    for n in range(4):
        product = jnp.dot(table_ref[n], strip, preferred_element_type=F32)
        out_ref[n, :STRIP] = (product[:STRIP, :STRIP] - product[STRIP:, STRIP:]).astype(BF16)
        out_ref[n, STRIP:] = (product[:STRIP, STRIP:] + product[STRIP:, :STRIP]).astype(BF16)


def place_kernel(place_ref, parts_ref, out_ref, scratch_ref):
    place = place_ref[0] & (SUBGRID - 1)
    scratch_ref[...] = jnp.zeros_like(scratch_ref)
    for part in range(2):
        rows = slice(STRIP * part, STRIP * (part + 1))
        total = parts_ref[0, rows, :].astype(F32)
        for n in range(1, 4):
            total += parts_ref[n, rows, :].astype(F32)
        scratch_ref[part, pl.ds(place, STRIP), :] = total
    out_ref[:, STRIP:, :] = scratch_ref[:, STRIP:SUBGRID, :]
    out_ref[:, :STRIP, :] = scratch_ref[:, :STRIP, :] + scratch_ref[:, SUBGRID:, :]


def call(kernel, specs, shape, dtype, scratch=(), flops=0, moved=1 << 20):
    return pl.pallas_call(
        kernel,
        out_shape=jax.ShapeDtypeStruct(shape, dtype),
        in_specs=specs,
        out_specs=VMEM,
        scratch_shapes=list(scratch),
        compiler_params=pltpu.CompilerParams(vmem_limit_bytes=24 * 1024 * 1024),
        cost_estimate=pl.CostEstimate(flops=flops, bytes_accessed=moved, transcendentals=0),
    )


def on_device(
    facets, row_taper, column_taper, column_place, row_offset, column_offset, slot_subgrid
):
    base = jnp.asarray(base_table())
    turned_scratch = pltpu.VMEM((2, STRIP, HALF), F32)
    own = call(prepare_kernel, [VMEM] * 3, (2 * STRIP, HALF), BF16)(
        facets, row_taper.reshape(1, HALF), column_taper.reshape(32, STRIP)
    )
    other = lax.ppermute(own, "core", [(0, 1), (1, 0)])
    encode = call(
        encode_kernel, [SMEM, VMEM], (8, 2 * STRIP, 2 * HALF), BF16, [turned_scratch], moved=3 << 20
    )(row_offset, base)
    decode = call(
        decode_kernel, [SMEM, SMEM, VMEM], (4, 2 * STRIP, 4 * HALF), BF16, [turned_scratch], moved=3 << 20
    )(slot_subgrid, column_offset, base)
    shares = call(strip_kernel, [VMEM] * 3, (8, STRIP, 2 * STRIP), BF16, flops=1 << 29)(
        own, other, encode
    )
    shares = lax.all_to_all(shares, ("xh", "y"), 0, 0)
    strip = call(sum_kernel, [VMEM], (8, STRIP, 2 * STRIP), BF16)(shares)
    strips = lax.all_to_all(strip, ("xl", "zl"), 0, 0)
    partial = call(subgrid_kernel, [VMEM] * 2, (4, 2 * STRIP, STRIP), BF16, flops=1 << 29)(
        strips, decode
    )
    received = lax.all_to_all(partial, "zh", 0, 0)
    subgrid = call(
        place_kernel,
        [SMEM, VMEM],
        (2, SUBGRID, STRIP),
        F32,
        [pltpu.VMEM((2, SUBGRID + STRIP, STRIP), F32)],
    )(column_place, received)
    return subgrid.reshape(1, 1, 2, SUBGRID, STRIP)


def solution(mesh):
    split = Mesh(mesh.devices.reshape(SIZES), SPLIT)
    in_specs = (P(None, COL, FAC), P(COL), P(), P(), P(), P(), P())
    return jax.shard_map(
        on_device,
        mesh=split,
        in_specs=in_specs,
        out_specs=P(COL, FAC, None, None, None),
        check_vma=False,
    )
```

profile of v0, /device:TPU:2, one launch (start us, length us, event | category | flops | bytes accessed | tf_op | source)
XLA Modules:
  0.0 80.0 jit_solution(15539901425074183602)
XLA Ops:
  0.0 0.9 %copy-done.2 = bf16[2,256,128]{2,1,0:T(8,128)(2,1)S(1)} copy-done((bf16[2,256,128]{2,1,0:T(8,128)(2,1)S(1)}, bf16[2,256,128]{2,1,0:T(8,128)(2,1)}, u32[]{:S(2)}) %copy-start.2) | copy-done | bytes 131096
  0.9 0.7 copy-done.3
  1.6 0.7 copy-done.5
  2.3 0.1 shard_map.82.own_ref
  2.4 1.9 %collective-permute-start = (bf16[256,256]{1,0:T(8,128)(2,1)S(1)}, bf16[256,256]{1,0:T(8,128)(2,1)S(1)}, u32[]{:S(2)}, u32[]{:S(2)}) collective-permute-start(bf16[256,256]{1,0:T(8,128)(2,1)S(1)} %shard_map.82.own_ref), channel_id=1, source_target_pairs={{0,32},{32,0},{1,33},{33,1},{2,34},{34,2},{3,35},{35,3},{4,36},{36... | collective-permute-start | bytes 393224 | tf_op jit(solution)/shard_map/ppermute | solution.py:158
  4.4 0.0 copy-start
  4.4 0.9 %copy-done = f32[2,128,256]{2,1,0:T(8,128)S(1)} copy-done((f32[2,128,256]{2,1,0:T(8,128)S(1)}, f32[2,128,256]{2,1,0:T(8,128)}, u32[]{:S(2)}) %copy-start) | copy-done | bytes 262168
  5.3 0.7 copy-done.6
  6.0 1.2 %shard_map.83.table_ref = bf16[8,256,512]{2,1,0:T(8,128)(2,1)S(1)} custom-call(s32[16]{0:T(128)S(1)} %copy-done.6, f32[2,128,256]{2,1,0:T(8,128)S(1)} %copy-done), custom_call_target="tpu_custom_call" | custom-call | bytes 3145728 | tf_op jit(solution)/shard_map/pallas_call | solution.py:159
  7.2 0.0 collective-permute-done.other_ref
  7.2 0.7 shard_map.84
  8.0 0.0 copy-start.1
  8.0 0.0 copy-start.4
  8.0 0.0 copy-start.7
  8.0 18.0 %all_to_all.15.parts_ref = bf16[8,128,256]{2,1,0:T(8,128)(2,1)S(1)} all-to-all(bf16[8,128,256]{2,1,0:T(8,128)(2,1)S(1)} %shard_map.84), channel_id=1, replica_groups=mesh['xh'=2,'y'=4,'core'=2,'xl'=2,'zh'=4,'zl'=4] {'xh','y'}, dimensions={0} | all-to-all | bytes 1048576 | tf_op jit(solution)/shard_map/all_to_all | solution.py:168
  26.0 0.9 %shard_map.85 = bf16[8,128,256]{2,1,0:T(8,128)(2,1)} custom-call(bf16[8,128,256]{2,1,0:T(8,128)(2,1)S(1)} %all_to_all.15.parts_ref), custom_call_target="tpu_custom_call" | custom-call | bytes 1048576 | tf_op jit(solution)/shard_map/pallas_call | solution.py:169
  26.9 7.4 %all-to-all-start.1 = ((bf16[8,128,256]{2,1,0:T(8,128)(2,1)}), bf16[8,128,256]{2,1,0:T(8,128)(2,1)S(1)}, u32[]{:S(2)}, u32[]{:S(2)}) async-start(bf16[8,128,256]{2,1,0:T(8,128)(2,1)} %shard_map.85), calls=%async_computation.1 | async-start | bytes 1048576 | tf_op jit(solution)/shard_map/all_to_all | solution.py:170
  34.2 0.0 copy-done.1
  34.3 1.5 %shard_map.86.table_ref = bf16[4,256,1024]{2,1,0:T(8,128)(2,1)S(1)} custom-call(s32[16,32]{1,0:T(8,128)S(1)} %copy-done.4, s32[32]{0:T(128)S(1)} %copy-done.7, f32[2,128,256]{2,1,0:T(8,128)S(1)} %copy-done.1), custom_call_target="tpu_custom_call" | custom-call | bytes 3145728 | tf_op jit(solution)/shard_map/pallas_call | solution.py:162
  35.8 11.1 %all-to-all-done.1.strip_ref = bf16[8,128,256]{2,1,0:T(8,128)(2,1)S(1)} async-done(((bf16[8,128,256]{2,1,0:T(8,128)(2,1)}), bf16[8,128,256]{2,1,0:T(8,128)(2,1)S(1)}, u32[]{:S(2)}, u32[]{:S(2)}) %all-to-all-start.1) | async-done | bytes 524320 | tf_op jit(solution)/shard_map/all_to_all | solution.py:170
  46.9 1.4 %shard_map.87 = bf16[4,256,128]{2,1,0:T(8,128)(2,1)} custom-call(bf16[8,128,256]{2,1,0:T(8,128)(2,1)S(1)} %all-to-all-done.1.strip_ref, bf16[4,256,1024]{2,1,0:T(8,128)(2,1)S(1)} %shard_map.86.table_ref), custom_call_target="tpu_custom_call" | custom-call | flops 536870912 | bytes 1048576 | tf_op jit(solution)/shard_map/pallas_call | solution.py:171
  48.3 12.8 %all-to-all-start.2 = ((bf16[4,256,128]{2,1,0:T(8,128)(2,1)}), bf16[4,256,128]{2,1,0:T(8,128)(2,1)S(1)}, u32[]{:S(2)}, u32[]{:S(2)}) async-start(bf16[4,256,128]{2,1,0:T(8,128)(2,1)} %shard_map.87), calls=%async_computation.2 | async-start | bytes 524288 | tf_op jit(solution)/shard_map/all_to_all | solution.py:174
  61.8 17.3 %all-to-all-done.2.parts_ref = bf16[4,256,128]{2,1,0:T(8,128)(2,1)S(1)} async-done(((bf16[4,256,128]{2,1,0:T(8,128)(2,1)}), bf16[4,256,128]{2,1,0:T(8,128)(2,1)S(1)}, u32[]{:S(2)}, u32[]{:S(2)}) %all-to-all-start.2) | async-done | bytes 262176 | tf_op jit(solution)/shard_map/all_to_all | solution.py:174
  79.1 0.9 %shard_map.88 = f32[2,512,128]{2,1,0:T(8,128)} custom-call(s32[1]{0:T(128)S(6)} %copy.9.place_ref, bf16[4,256,128]{2,1,0:T(8,128)(2,1)S(1)} %all-to-all-done.2.parts_ref), custom_call_target="tpu_custom_call" | custom-call | bytes 1048576 | tf_op jit(solution)/shard_map/pallas_call | solution.py:175
  (6 shorter events, 0.0 us)
Async XLA Ops:
  0.0 0.9 %copy-start.2 = (bf16[2,256,128]{2,1,0:T(8,128)(2,1)S(1)}, bf16[2,256,128]{2,1,0:T(8,128)(2,1)}, u32[]{:S(2)}) copy-start(bf16[2,256,128]{2,1,0:T(8,128)(2,1)} %facets_ref.1) | copy-start | bytes 393220
  0.9 0.7 copy-start.3
  1.6 0.7 copy-start.5
  2.4 4.8 %collective-permute-start = (bf16[256,256]{1,0:T(8,128)(2,1)S(1)}, bf16[256,256]{1,0:T(8,128)(2,1)S(1)}, u32[]{:S(2)}, u32[]{:S(2)}) collective-permute-start(bf16[256,256]{1,0:T(8,128)(2,1)S(1)} %shard_map.82.own_ref), channel_id=1, source_target_pairs={{0,32},{32,0},{1,33},{33,1},{2,34},{34,2},{3,35},{35,3},{4,36},{36... | collective-permute-start | bytes 393224 | tf_op jit(solution)/shard_map/ppermute | solution.py:158
  4.4 1.0 %copy-start = (f32[2,128,256]{2,1,0:T(8,128)S(1)}, f32[2,128,256]{2,1,0:T(8,128)}, u32[]{:S(2)}) copy-start(f32[2,128,256]{2,1,0:T(8,128)} %constant.2.clone.base_ref) | copy-start | bytes 786436
  5.3 0.7 copy-start.6
  8.0 26.3 %copy-start.1 = (f32[2,128,256]{2,1,0:T(8,128)S(1)}, f32[2,128,256]{2,1,0:T(8,128)}, u32[]{:S(2)}) copy-start(f32[2,128,256]{2,1,0:T(8,128)} %constant.2.clone.base_ref) | copy-start | bytes 786436
  8.0 26.3 %copy-start.4 = (s32[16,32]{1,0:T(8,128)S(1)}, s32[16,32]{1,0:T(8,128)}, u32[]{:S(2)}) copy-start(s32[16,32]{1,0:T(8,128)} %slot_ref.1) | copy-start | bytes 6148
  8.0 26.3 %copy-start.7 = (s32[32]{0:T(128)S(1)}, s32[32]{0:T(128)}, u32[]{:S(2)}) copy-start(s32[32]{0:T(128)} %offset_ref.1) | copy-start | bytes 388
  26.9 20.1 %all-to-all-start.1 = ((bf16[8,128,256]{2,1,0:T(8,128)(2,1)}), bf16[8,128,256]{2,1,0:T(8,128)(2,1)S(1)}, u32[]{:S(2)}, u32[]{:S(2)}) async-start(bf16[8,128,256]{2,1,0:T(8,128)(2,1)} %shard_map.85), calls=%async_computation.1 | async-start | bytes 1048576 | tf_op jit(solution)/shard_map/all_to_all | solution.py:170
  48.3 30.8 %all-to-all-start.2 = ((bf16[4,256,128]{2,1,0:T(8,128)(2,1)}), bf16[4,256,128]{2,1,0:T(8,128)(2,1)S(1)}, u32[]{:S(2)}, u32[]{:S(2)}) async-start(bf16[4,256,128]{2,1,0:T(8,128)(2,1)} %shard_map.87), calls=%async_computation.2 | async-start | bytes 524288 | tf_op jit(solution)/shard_map/all_to_all | solution.py:174
where the time goes:
time: 80.5 us; the launch traced here: 80 us
  waiting for transfers between devices  28.4 us (35%)
  starting transfers between devices  22.1 us (27%)
  blocking collectives  18 us (22%)
  Pallas kernels  6.82 us (8%)
  local copies, waits for them, and re-layouts  3.92 us (5%)
    all_to_all x1, blocking collectives, on_device(): shares = lax.all_to_all(shares, ('xh', 'y'), 0, 0)  18 us
    all_to_all x1, waiting for transfers between devices, on_device(): received = lax.all_to_all(partial, 'zh', 0, 0)  17.3 us
    all_to_all x1, starting transfers between devices, on_device(): received = lax.all_to_all(partial, 'zh', 0, 0)  12.8 us
    all_to_all x1, waiting for transfers between devices, on_device(): strips = lax.all_to_all(strip, ('xl', 'zl'), 0, 0)  11.1 us
    all_to_all x1, starting transfers between devices, on_device(): strips = lax.all_to_all(strip, ('xl', 'zl'), 0, 0)  7.36 us
    unnamed x16, local copies, waits for them, and re-layouts  3.92 us
    ppermute x1, starting transfers between devices, on_device(): other = lax.ppermute(own, 'core', [(0, 1), (1, 0)])  1.92 us
  transfers between devices with their start and end apart: 3, of which 2 were waited for; matrix products, arithmetic and copies ran while one was open for 0% of the time, Pallas kernels for 3%

commit v1 on v0

--- a/solution.py
+++ b/solution.py
@@ -1,3 +1,4 @@
+import functools
 import math
 
 import jax
@@ -19,7 +20,10 @@
 F32 = jnp.float32
 BF16 = jnp.bfloat16
 VMEM = pl.BlockSpec(memory_space=pltpu.VMEM)
+HBM = pl.BlockSpec(memory_space=pltpu.HBM)
 SMEM = pl.BlockSpec(memory_space=pltpu.SMEM)
+ENCODE = slice(2 * STRIP, 2 * STRIP + 8)
+DECODE = slice(2 * STRIP + 8, 2 * STRIP + 16)
 NT = (((1,), (1,)), ((), ()))
 
 
@@ -36,26 +40,29 @@
     return jnp.cos(angle), -jnp.sin(angle)
 
 
-def turned(base_ref, turned_ref, block):
+def turned(pack_ref, turned_ref, block):
     k = lax.broadcasted_iota(jnp.int32, (16, HALF), 0)
     real, imag = unit((k * block & 15) * HALF)
     for row in range(0, STRIP, 16):
         rows = pl.ds(row, 16)
-        base_real, base_imag = base_ref[0, rows, :], base_ref[1, rows, :]
+        base_real, base_imag = pack_ref[rows, :], pack_ref[pl.ds(STRIP + row, 16), :]
         turned_ref[0, rows, :] = base_real * real - base_imag * imag
         turned_ref[1, rows, :] = base_real * imag + base_imag * real
 
 
-def fill_tables(starts, blocks, base_ref, out_ref, turned_ref):
-    count = len(starts)
-    padded = 8
-    row = lax.broadcasted_iota(jnp.int32, (padded, HALF), 0)
-    lane = lax.broadcasted_iota(jnp.int32, (padded, HALF), 1)
-    first = jnp.zeros((padded, HALF), jnp.int32)
+def spread(starts):
+    row = lax.broadcasted_iota(jnp.int32, (8, HALF), 0)
+    first = jnp.zeros((8, HALF), jnp.int32)
     for n, start in enumerate(starts):
         first = jnp.where(row == n, start, first)
+    return first.astype(F32)
+
+
+def fill_tables(pack_ref, firsts, count, blocks, out_ref, turned_ref):
+    lane = lax.broadcasted_iota(jnp.int32, (8, HALF), 1)
+    first = pack_ref[firsts].astype(jnp.int32)
     for c, block in enumerate(blocks):
-        turned(base_ref, turned_ref, block)
+        turned(pack_ref, turned_ref, block)
         real, imag = unit(first * (block * HALF + lane) & (FACET - 1))
         for k in range(0, STRIP, 16):
             rows = pl.ds(k, 16)
@@ -70,28 +77,69 @@
                 ).astype(BF16)
 
 
-def prepare_kernel(facets_ref, row_ref, column_ref, out_ref):
-    fac = (lax.axis_index("xl") * 4 + lax.axis_index("zh")) * 4 + lax.axis_index("zl")
-    column = column_ref[pl.ds(fac, 1), :]
+def prepare_kernel(
+    facets_hbm,
+    row_hbm,
+    column_hbm,
+    row_offset_hbm,
+    offset_hbm,
+    slot_hbm,
+    base_hbm,
+    out_ref,
+    pack_ref,
+    facets_ref,
+    row_ref,
+    column_ref,
+    row_offset_ref,
+    offset_ref,
+    slot_ref,
+    sems,
+):
+    copies = [
+        pltpu.make_async_copy(source, target, sems.at[n])
+        for n, (source, target) in enumerate(
+            [
+                (facets_hbm, facets_ref),
+                (row_hbm, row_ref),
+                (column_hbm, column_ref),
+                (row_offset_hbm, row_offset_ref),
+                (offset_hbm, offset_ref),
+                (slot_hbm, slot_ref),
+                (base_hbm, pack_ref.at[pl.ds(0, 2 * STRIP)]),
+            ]
+        )
+    ]
+    for copy in copies:
+        copy.start()
+    core, xl, zh, zl = (lax.axis_index(name) for name in ("core", "xl", "zh", "zl"))
+    pair = lax.axis_index("xh") * 4 + lax.axis_index("y")
+    for copy in copies[3:6]:
+        copy.wait()
+    pack_ref[ENCODE] = spread([row_offset_ref[2 * n + core] for n in range(8)])
+    pack_ref[DECODE] = spread(
+        [
+            offset_ref[slot_ref[2 * pair + core, 16 * xl + 4 * n + ((zl - zh + n) & 3)] & 31]
+            for n in range(4)
+        ]
+    )
+    for copy in copies[:3]:
+        copy.wait()
+    column = column_ref[pl.ds((xl * 4 + zh) * 4 + zl, 1), :]
     for part in range(2):
         scaled = facets_ref[part].astype(F32) * column
         out_ref[STRIP * part : STRIP * (part + 1), :] = (scaled.T * row_ref[...]).astype(BF16)
-
-
-def encode_kernel(row_offset_ref, base_ref, out_ref, turned_ref):
+    copies[6].wait()
+
+
+def encode_kernel(pack_ref, out_ref, turned_ref):
     core = lax.axis_index("core")
     pair = lax.axis_index("xh") * 4 + lax.axis_index("y")
-    starts = [row_offset_ref[2 * n + core] for n in range(8)]
-    fill_tables(starts, [2 * pair + core, 2 * pair + 1 - core], base_ref, out_ref, turned_ref)
-
-
-def decode_kernel(slot_ref, offset_ref, base_ref, out_ref, turned_ref):
-    column = (lax.axis_index("xh") * 4 + lax.axis_index("y")) * 2 + lax.axis_index("core")
-    zh = lax.axis_index("zh")
-    slot = lax.axis_index("xl") * 16 + lax.axis_index("zl")
-    starts = [offset_ref[slot_ref[column, slot + 4 * n]] for n in range(4)]
-    blocks = [2 * zh, 2 * zh + 1, 2 * zh + 8, 2 * zh + 9]
-    fill_tables(starts, blocks, base_ref, out_ref, turned_ref)
+    fill_tables(pack_ref, ENCODE, 8, [2 * pair + core, 2 * pair + 1 - core], out_ref, turned_ref)
+
+
+def decode_kernel(xl, pack_ref, out_ref, turned_ref):
+    block = 8 * xl + 2 * lax.axis_index("zh")
+    fill_tables(pack_ref, DECODE, 4, [block, block + 1], out_ref, turned_ref)
 
 
 def strip_kernel(own_ref, other_ref, table_ref, out_ref):
@@ -114,10 +162,13 @@
         out_ref[n] = total
 
 
-def subgrid_kernel(strip_ref, table_ref, out_ref):
-    strip = strip_ref[...].reshape(8 * STRIP, 2 * STRIP)
+def subgrid_kernel(strip_ref, low_ref, high_ref, out_ref):
+    low = strip_ref[:4].reshape(4 * STRIP, 2 * STRIP)
+    high = strip_ref[4:].reshape(4 * STRIP, 2 * STRIP)
     for n in range(4):
-        product = jnp.dot(table_ref[n], strip, preferred_element_type=F32)
+        product = jnp.dot(low_ref[n], low, preferred_element_type=F32) + jnp.dot(
+            high_ref[n], high, preferred_element_type=F32
+        )
         out_ref[n, :STRIP] = (product[:STRIP, :STRIP] - product[STRIP:, STRIP:]).astype(BF16)
         out_ref[n, STRIP:] = (product[:STRIP, STRIP:] + product[STRIP:, :STRIP]).astype(BF16)
 
@@ -147,31 +198,69 @@
     )
 
 
+def prepare(*operands):
+    return pl.pallas_call(
+        prepare_kernel,
+        out_shape=(
+            jax.ShapeDtypeStruct((2 * STRIP, HALF), BF16),
+            jax.ShapeDtypeStruct((2 * STRIP + 16, HALF), F32),
+        ),
+        in_specs=[HBM] * 7,
+        out_specs=(VMEM, VMEM),
+        scratch_shapes=[
+            pltpu.VMEM((2, HALF, STRIP), BF16),
+            pltpu.VMEM((1, HALF), F32),
+            pltpu.VMEM((32, STRIP), F32),
+            pltpu.SMEM((16,), jnp.int32),
+            pltpu.SMEM((32,), jnp.int32),
+            pltpu.SMEM((16, 32), jnp.int32),
+            pltpu.SemaphoreType.DMA((7,)),
+        ],
+        compiler_params=pltpu.CompilerParams(vmem_limit_bytes=60 * 1024 * 1024),
+        cost_estimate=pl.CostEstimate(flops=0, bytes_accessed=1 << 20, transcendentals=0),
+    )(*operands)
+
+
+SPREAD = [[16 * xl + 4 * n + (s + n) % 4 for n in range(4)] for xl in range(2) for s in range(4)]
+
+
 def on_device(
     facets, row_taper, column_taper, column_place, row_offset, column_offset, slot_subgrid
 ):
-    base = jnp.asarray(base_table())
-    turned_scratch = pltpu.VMEM((2, STRIP, HALF), F32)
-    own = call(prepare_kernel, [VMEM] * 3, (2 * STRIP, HALF), BF16)(
-        facets, row_taper.reshape(1, HALF), column_taper.reshape(32, STRIP)
+    turned_scratch = [pltpu.VMEM((2, STRIP, HALF), F32)]
+    own, pack = prepare(
+        facets,
+        row_taper.reshape(1, HALF),
+        column_taper.reshape(32, STRIP),
+        row_offset,
+        column_offset,
+        slot_subgrid,
+        jnp.asarray(base_table().reshape(2 * STRIP, HALF)),
     )
     other = lax.ppermute(own, "core", [(0, 1), (1, 0)])
     encode = call(
-        encode_kernel, [SMEM, VMEM], (8, 2 * STRIP, 2 * HALF), BF16, [turned_scratch], moved=3 << 20
-    )(row_offset, base)
-    decode = call(
-        decode_kernel, [SMEM, SMEM, VMEM], (4, 2 * STRIP, 4 * HALF), BF16, [turned_scratch], moved=3 << 20
-    )(slot_subgrid, column_offset, base)
+        encode_kernel, [VMEM], (8, 2 * STRIP, 2 * HALF), BF16, turned_scratch, moved=3 << 20
+    )(pack)
     shares = call(strip_kernel, [VMEM] * 3, (8, STRIP, 2 * STRIP), BF16, flops=1 << 29)(
         own, other, encode
     )
-    shares = lax.all_to_all(shares, ("xh", "y"), 0, 0)
+
+    def decode(xl, pack):
+        kernel = functools.partial(decode_kernel, xl)
+        shape = (4, 2 * STRIP, 2 * HALF)
+        return call(kernel, [VMEM], shape, BF16, turned_scratch, moved=2 << 20)(pack)
+
+    shares, pack = lax.optimization_barrier((shares, pack))
+    low = decode(0, pack)
+    shares, low = lax.optimization_barrier((lax.all_to_all(shares, ("xh", "y"), 0, 0), low))
     strip = call(sum_kernel, [VMEM], (8, STRIP, 2 * STRIP), BF16)(shares)
+    strip, pack = lax.optimization_barrier((strip, pack))
+    high = decode(1, pack)
     strips = lax.all_to_all(strip, ("xl", "zl"), 0, 0)
-    partial = call(subgrid_kernel, [VMEM] * 2, (4, 2 * STRIP, STRIP), BF16, flops=1 << 29)(
-        strips, decode
-    )
-    received = lax.all_to_all(partial, "zh", 0, 0)
+    partial = call(subgrid_kernel, [VMEM] * 3, (4, 2 * STRIP, STRIP), BF16, flops=1 << 29)(
+        strips, low, high
+    )
+    received = lax.all_to_all(partial, FAC, 0, 0, axis_index_groups=SPREAD)
     subgrid = call(
         place_kernel,
         [SMEM, VMEM],

time: 80.5 us -> 76.6 us (0.952)
  the two profiles are of different devices: /device:TPU:2 before, /device:TPU:70 now
where the time goes in v1:
time: 76.6 us; the launch traced here: 76.1 us
  waiting for transfers between devices  37.9 us (49%)
  starting transfers between devices  28.2 us (37%)
  Pallas kernels  8.15 us (11%)
  local copies, waits for them, and re-layouts  1.17 us (2%)
    all_to_all x1, waiting for transfers between devices, on_device(): received = lax.all_to_all(partial, FAC, 0, 0, axis_index_groups=SPREAD)  17.4 us
    all_to_all x1, starting transfers between devices, on_device(): received = lax.all_to_all(partial, FAC, 0, 0, axis_index_groups=SPREAD)  12.4 us
    all_to_all x1, waiting for transfers between devices, on_device(): strips = lax.all_to_all(strip, ('xl', 'zl'), 0, 0)  11.6 us
    all_to_all x1, waiting for transfers between devices, on_device(): lax.all_to_all(shares, ('xh', 'y'), 0, 0)  8.85 us
    all_to_all x1, starting transfers between devices, on_device(): lax.all_to_all(shares, ('xh', 'y'), 0, 0)  7.43 us
    all_to_all x1, starting transfers between devices, on_device(): strips = lax.all_to_all(strip, ('xl', 'zl'), 0, 0)  6.45 us
    pallas_call x1, Pallas kernels, prepare(): pl.pallas_call(prepare_kernel, out_shape=(jax.ShapeDtypeStruct((2 * STRIP...  1.92 us
    ppermute x1, starting transfers between devices, on_device(): other = lax.ppermute(own, 'core', [(0, 1), (1, 0)])  1.92 us
  transfers between devices with their start and end apart: 4, of which 3 were waited for; matrix products, arithmetic and copies ran while one was open for 0% of the time, Pallas kernels for 2%

profile of v1, /device:TPU:70, one launch (start us, length us, event | category | flops | bytes accessed | tf_op | source)
XLA Modules:
  0.0 76.1 jit_solution(9179447038458451427)
XLA Ops:
  0.0 1.9 %shard_map.82 = (bf16[256,256]{1,0:T(8,128)(2,1)}, f32[272,256]{1,0:T(8,128)}) custom-call(bf16[2,256,128]{2,1,0:T(8,128)(2,1)} %facets_hbm.1, f32[1,256]{1,0:T(1,128)} %bitcast.4, f32[32,128]{1,0:T(8,128)} %bitcast.3, s32[16]{0:T(128)} %row_offset_hbm.1, s32[32]{0:T(128)} %offset_hbm.1, s32[16,32]{1,0:T(8,128)} %slot_hbm.1, f32[256,256]{1,0:T(8,128)} %constant.2.clone.base_hbm), custom_call_target="tpu_custom_call" | custom-call | bytes 1048576 | tf_op jit(solution)/shard_map/pallas_call | solution.py:202
  1.9 1.9 %collective-permute-start = (bf16[256,256]{1,0:T(8,128)(2,1)}, bf16[256,256]{1,0:T(8,128)(2,1)S(1)}, u32[]{:S(2)}, u32[]{:S(2)}) collective-permute-start(bf16[256,256]{1,0:T(8,128)(2,1)} %get-tuple-element.13.own_ref), channel_id=1, source_target_pairs={{0,32},{32,0},{1,33},{33,1},{2,34},{34,2},{3,35},{35,3},{4,36},{36... | collective-permute-start | bytes 393224 | tf_op jit(solution)/shard_map/ppermute | solution.py:240
  3.9 0.0 copy-start
  3.9 0.9 %copy-done = f32[272,256]{1,0:T(8,128)S(1)} copy-done((f32[272,256]{1,0:T(8,128)S(1)}, f32[272,256]{1,0:T(8,128)}, u32[]{:S(2)}) %copy-start) | copy-done | bytes 278552
  4.8 0.0 copy-start.2
  4.8 0.7 shard_map.83.table_ref
  5.5 0.0 copy-start.1
  5.5 0.0 collective-permute-done.other_ref
  5.5 0.2 copy-done.2
  5.7 1.5 %shard_map.84 = bf16[8,128,256]{2,1,0:T(8,128)(2,1)} custom-call(bf16[256,256]{1,0:T(8,128)(2,1)S(1)} %copy-done.2, bf16[256,256]{1,0:T(8,128)(2,1)S(1)} %collective-permute-done.other_ref, bf16[8,256,512]{2,1,0:T(8,128)(2,1)S(1)} %shard_map.83.table_ref), custom_call_target="tpu_custom_call" | custom-call | flops 536870912 | bytes 1048576 | tf_op jit(solution)/shard_map/pallas_call | solution.py:244
  7.3 7.4 %all-to-all-start = ((bf16[8,128,256]{2,1,0:T(8,128)(2,1)}), bf16[8,128,256]{2,1,0:T(8,128)(2,1)S(1)}, u32[]{:S(2)}, u32[]{:S(2)}) async-start(bf16[8,128,256]{2,1,0:T(8,128)(2,1)} %shard_map.84), calls=%async_computation | async-start | bytes 1048576 | tf_op jit(solution)/shard_map/all_to_all | solution.py:255
  14.7 0.0 copy-done.1
  14.7 0.4 shard_map.85.low_ref
  15.1 8.8 %all-to-all-done.parts_ref = bf16[8,128,256]{2,1,0:T(8,128)(2,1)S(1)} async-done(((bf16[8,128,256]{2,1,0:T(8,128)(2,1)}), bf16[8,128,256]{2,1,0:T(8,128)(2,1)S(1)}, u32[]{:S(2)}, u32[]{:S(2)}) %all-to-all-start) | async-done | bytes 524320 | tf_op jit(solution)/shard_map/all_to_all | solution.py:255
  24.0 0.9 %shard_map.86 = bf16[8,128,256]{2,1,0:T(8,128)(2,1)} custom-call(bf16[8,128,256]{2,1,0:T(8,128)(2,1)S(1)} %all-to-all-done.parts_ref), custom_call_target="tpu_custom_call" | custom-call | bytes 1048576 | tf_op jit(solution)/shard_map/pallas_call | solution.py:256
  24.8 6.5 %all-to-all-start.1 = ((bf16[8,128,256]{2,1,0:T(8,128)(2,1)}), bf16[8,128,256]{2,1,0:T(8,128)(2,1)S(1)}, u32[]{:S(2)}, u32[]{:S(2)}) async-start(bf16[8,128,256]{2,1,0:T(8,128)(2,1)} %shard_map.86), calls=%async_computation.1 | async-start | bytes 1048576 | tf_op jit(solution)/shard_map/all_to_all | solution.py:259
  31.3 0.4 shard_map.87.high_ref
  31.7 11.6 %all-to-all-done.1.strip_ref = bf16[8,128,256]{2,1,0:T(8,128)(2,1)S(1)} async-done(((bf16[8,128,256]{2,1,0:T(8,128)(2,1)}), bf16[8,128,256]{2,1,0:T(8,128)(2,1)S(1)}, u32[]{:S(2)}, u32[]{:S(2)}) %all-to-all-start.1) | async-done | bytes 524320 | tf_op jit(solution)/shard_map/all_to_all | solution.py:259
  43.4 1.4 %shard_map.88 = bf16[4,256,128]{2,1,0:T(8,128)(2,1)} custom-call(bf16[8,128,256]{2,1,0:T(8,128)(2,1)S(1)} %all-to-all-done.1.strip_ref, bf16[4,256,512]{2,1,0:T(8,128)(2,1)S(1)} %shard_map.85.low_ref, bf16[4,256,512]{2,1,0:T(8,128)(2,1)S(1)} %shard_map.87.high_ref), custom_call_target="tpu_custom_call" | custom-call | flops 536870912 | bytes 1048576 | tf_op jit(solution)/shard_map/pallas_call | solution.py:260
  44.8 12.4 %all-to-all-start.2 = ((bf16[4,256,128]{2,1,0:T(8,128)(2,1)}), bf16[4,256,128]{2,1,0:T(8,128)(2,1)S(1)}, u32[]{:S(2)}, u32[]{:S(2)}) async-start(bf16[4,256,128]{2,1,0:T(8,128)(2,1)} %shard_map.88), calls=%async_computation.2 | async-start | bytes 524288 | tf_op jit(solution)/shard_map/all_to_all | solution.py:263
  57.8 17.4 %all-to-all-done.2.parts_ref = bf16[4,256,128]{2,1,0:T(8,128)(2,1)S(1)} async-done(((bf16[4,256,128]{2,1,0:T(8,128)(2,1)}), bf16[4,256,128]{2,1,0:T(8,128)(2,1)S(1)}, u32[]{:S(2)}, u32[]{:S(2)}) %all-to-all-start.2) | async-done | bytes 262176 | tf_op jit(solution)/shard_map/all_to_all | solution.py:263
  75.2 0.9 %shard_map.89 = f32[2,512,128]{2,1,0:T(8,128)} custom-call(s32[1]{0:T(128)S(6)} %copy.9.place_ref, bf16[4,256,128]{2,1,0:T(8,128)(2,1)S(1)} %all-to-all-done.2.parts_ref), custom_call_target="tpu_custom_call" | custom-call | bytes 1048576 | tf_op jit(solution)/shard_map/pallas_call | solution.py:264
Async XLA Ops:
  1.9 3.6 %collective-permute-start = (bf16[256,256]{1,0:T(8,128)(2,1)}, bf16[256,256]{1,0:T(8,128)(2,1)S(1)}, u32[]{:S(2)}, u32[]{:S(2)}) collective-permute-start(bf16[256,256]{1,0:T(8,128)(2,1)} %get-tuple-element.13.own_ref), channel_id=1, source_target_pairs={{0,32},{32,0},{1,33},{33,1},{2,34},{34,2},{3,35},{35,3},{4,36},{36... | collective-permute-start | bytes 393224 | tf_op jit(solution)/shard_map/ppermute | solution.py:240
  3.9 1.0 %copy-start = (f32[272,256]{1,0:T(8,128)S(1)}, f32[272,256]{1,0:T(8,128)}, u32[]{:S(2)}) copy-start(f32[272,256]{1,0:T(8,128)} %get-tuple-element.20.pack_ref) | copy-start | bytes 835588
  4.8 0.9 %copy-start.2 = (bf16[256,256]{1,0:T(8,128)(2,1)S(1)}, bf16[256,256]{1,0:T(8,128)(2,1)}, u32[]{:S(2)}) copy-start(bf16[256,256]{1,0:T(8,128)(2,1)} %get-tuple-element.13.own_ref) | copy-start | bytes 393220
  5.5 9.2 %copy-start.1 = (f32[272,256]{1,0:T(8,128)S(1)}, f32[272,256]{1,0:T(8,128)}, u32[]{:S(2)}) copy-start(f32[272,256]{1,0:T(8,128)} %get-tuple-element.20.pack_ref) | copy-start | bytes 835588
  7.3 16.7 %all-to-all-start = ((bf16[8,128,256]{2,1,0:T(8,128)(2,1)}), bf16[8,128,256]{2,1,0:T(8,128)(2,1)S(1)}, u32[]{:S(2)}, u32[]{:S(2)}) async-start(bf16[8,128,256]{2,1,0:T(8,128)(2,1)} %shard_map.84), calls=%async_computation | async-start | bytes 1048576 | tf_op jit(solution)/shard_map/all_to_all | solution.py:255
  24.8 18.5 %all-to-all-start.1 = ((bf16[8,128,256]{2,1,0:T(8,128)(2,1)}), bf16[8,128,256]{2,1,0:T(8,128)(2,1)S(1)}, u32[]{:S(2)}, u32[]{:S(2)}) async-start(bf16[8,128,256]{2,1,0:T(8,128)(2,1)} %shard_map.86), calls=%async_computation.1 | async-start | bytes 1048576 | tf_op jit(solution)/shard_map/all_to_all | solution.py:259
  44.8 30.5 %all-to-all-start.2 = ((bf16[4,256,128]{2,1,0:T(8,128)(2,1)}), bf16[4,256,128]{2,1,0:T(8,128)(2,1)S(1)}, u32[]{:S(2)}, u32[]{:S(2)}) async-start(bf16[4,256,128]{2,1,0:T(8,128)(2,1)} %shard_map.88), calls=%async_computation.2 | async-start | bytes 524288 | tf_op jit(solution)/shard_map/all_to_all | solution.py:263

commit v2 on v1

--- a/solution.py
+++ b/solution.py
@@ -48,6 +48,12 @@
         base_real, base_imag = pack_ref[rows, :], pack_ref[pl.ds(STRIP + row, 16), :]
         turned_ref[0, rows, :] = base_real * real - base_imag * imag
         turned_ref[1, rows, :] = base_real * imag + base_imag * real
+
+
+def position():
+    core, xl, zh, zl = (lax.axis_index(name) for name in ("core", "xl", "zh", "zl"))
+    place = (4 * zh + zl - 2 * core) & 15
+    return core, xl, place >> 2, place & 3
 
 
 def spread(starts):
@@ -85,16 +91,22 @@
     offset_hbm,
     slot_hbm,
     base_hbm,
-    out_ref,
-    pack_ref,
+    out_hbm,
+    pack_hbm,
     facets_ref,
     row_ref,
     column_ref,
     row_offset_ref,
     offset_ref,
     slot_ref,
+    out_ref,
+    pack_ref,
     sems,
+    out_sems,
 ):
+    core, xl, line, step = position()
+    pair = lax.axis_index("xh") * 4 + lax.axis_index("y")
+    fac = (xl * 4 + lax.axis_index("zh")) * 4 + lax.axis_index("zl")
     copies = [
         pltpu.make_async_copy(source, target, sems.at[n])
         for n, (source, target) in enumerate(
@@ -111,24 +123,33 @@
     ]
     for copy in copies:
         copy.start()
-    core, xl, zh, zl = (lax.axis_index(name) for name in ("core", "xl", "zh", "zl"))
-    pair = lax.axis_index("xh") * 4 + lax.axis_index("y")
+    for copy in copies[:3]:
+        copy.wait()
+    column = column_ref[pl.ds(fac, 1), :]
+    for part in range(2):
+        scaled = facets_ref[part].astype(F32) * column
+        out_ref[STRIP * part : STRIP * (part + 1), :] = (scaled.T * row_ref[...]).astype(BF16)
+    own_copy = pltpu.make_async_copy(out_ref, out_hbm, out_sems.at[0])
+    own_copy.start()
     for copy in copies[3:6]:
         copy.wait()
     pack_ref[ENCODE] = spread([row_offset_ref[2 * n + core] for n in range(8)])
     pack_ref[DECODE] = spread(
         [
-            offset_ref[slot_ref[2 * pair + core, 16 * xl + 4 * n + ((zl - zh + n) & 3)] & 31]
+            offset_ref[
+                slot_ref[
+                    2 * pair + core, 16 * xl + ((4 * n + 2 * core + ((step - line + n) & 3)) & 15)
+                ]
+                & 31
+            ]
             for n in range(4)
         ]
     )
-    for copy in copies[:3]:
-        copy.wait()
-    column = column_ref[pl.ds((xl * 4 + zh) * 4 + zl, 1), :]
-    for part in range(2):
-        scaled = facets_ref[part].astype(F32) * column
-        out_ref[STRIP * part : STRIP * (part + 1), :] = (scaled.T * row_ref[...]).astype(BF16)
     copies[6].wait()
+    pack_copy = pltpu.make_async_copy(pack_ref, pack_hbm, out_sems.at[1])
+    pack_copy.start()
+    own_copy.wait()
+    pack_copy.wait()
 
 
 def encode_kernel(pack_ref, out_ref, turned_ref):
@@ -138,11 +159,19 @@
 
 
 def decode_kernel(xl, pack_ref, out_ref, turned_ref):
-    block = 8 * xl + 2 * lax.axis_index("zh")
-    fill_tables(pack_ref, DECODE, 4, [block, block + 1], out_ref, turned_ref)
-
-
-def strip_kernel(own_ref, other_ref, table_ref, out_ref):
+    core, _, line, _ = position()
+    blocks = [8 * xl + ((2 * line + core + half) & 7) for half in range(2)]
+    fill_tables(pack_ref, DECODE, 4, blocks, out_ref, turned_ref)
+
+
+def sent(n, out_ref, out_hbm, sems):
+    copy = pltpu.make_async_copy(out_ref.at[n], out_hbm.at[n], sems.at[n])
+    copy.start()
+    return copy
+
+
+def strip_kernel(own_ref, other_ref, table_ref, out_hbm, out_ref, sems):
+    copies = []
     for n in range(8):
         product = lax.dot_general(
             own_ref[...], table_ref[n, :, :HALF], NT, preferred_element_type=F32
@@ -151,47 +180,64 @@
         )
         out_ref[n, :, :STRIP] = (product[:STRIP, :STRIP] - product[STRIP:, STRIP:]).astype(BF16)
         out_ref[n, :, STRIP:] = (product[:STRIP, STRIP:] + product[STRIP:, :STRIP]).astype(BF16)
-
-
-def sum_kernel(parts_ref, out_ref):
+        copies.append(sent(n, out_ref, out_hbm, sems))
+    for copy in copies:
+        copy.wait()
+
+
+def sum_kernel(parts_ref, out_hbm, total_ref, sems):
     total = parts_ref[0].astype(F32)
     for n in range(1, 8):
         total += parts_ref[n].astype(F32)
-    total = total.astype(BF16)
-    for n in range(8):
-        out_ref[n] = total
-
-
-def subgrid_kernel(strip_ref, low_ref, high_ref, out_ref):
+    total_ref[...] = total.astype(BF16)
+    copies = [pltpu.make_async_copy(total_ref, out_hbm.at[n], sems.at[n]) for n in range(8)]
+    for copy in copies:
+        copy.start()
+    for copy in copies:
+        copy.wait()
+
+
+def subgrid_kernel(strip_ref, low_ref, high_ref, out_hbm, out_ref, sems):
     low = strip_ref[:4].reshape(4 * STRIP, 2 * STRIP)
     high = strip_ref[4:].reshape(4 * STRIP, 2 * STRIP)
+    copies = []
     for n in range(4):
         product = jnp.dot(low_ref[n], low, preferred_element_type=F32) + jnp.dot(
             high_ref[n], high, preferred_element_type=F32
         )
         out_ref[n, :STRIP] = (product[:STRIP, :STRIP] - product[STRIP:, STRIP:]).astype(BF16)
         out_ref[n, STRIP:] = (product[:STRIP, STRIP:] + product[STRIP:, :STRIP]).astype(BF16)
-
-
-def place_kernel(place_ref, parts_ref, out_ref, scratch_ref):
+        copies.append(sent(n, out_ref, out_hbm, sems))
+    for copy in copies:
+        copy.wait()
+
+
+def place_kernel(place_ref, parts_ref, out_hbm, scratch_ref, sems):
     place = place_ref[0] & (SUBGRID - 1)
     scratch_ref[...] = jnp.zeros_like(scratch_ref)
+    copies = []
     for part in range(2):
         rows = slice(STRIP * part, STRIP * (part + 1))
         total = parts_ref[0, rows, :].astype(F32)
         for n in range(1, 4):
             total += parts_ref[n, rows, :].astype(F32)
         scratch_ref[part, pl.ds(place, STRIP), :] = total
-    out_ref[:, STRIP:, :] = scratch_ref[:, STRIP:SUBGRID, :]
-    out_ref[:, :STRIP, :] = scratch_ref[:, :STRIP, :] + scratch_ref[:, SUBGRID:, :]
-
-
-def call(kernel, specs, shape, dtype, scratch=(), flops=0, moved=1 << 20):
+        scratch_ref[part, :STRIP, :] += scratch_ref[part, SUBGRID:, :]
+        copy = pltpu.make_async_copy(
+            scratch_ref.at[part, pl.ds(0, SUBGRID)], out_hbm.at[part], sems.at[part]
+        )
+        copy.start()
+        copies.append(copy)
+    for copy in copies:
+        copy.wait()
+
+
+def call(kernel, specs, shape, dtype, scratch=(), flops=0, moved=1 << 20, out=VMEM):
     return pl.pallas_call(
         kernel,
         out_shape=jax.ShapeDtypeStruct(shape, dtype),
         in_specs=specs,
-        out_specs=VMEM,
+        out_specs=out,
         scratch_shapes=list(scratch),
         compiler_params=pltpu.CompilerParams(vmem_limit_bytes=24 * 1024 * 1024),
         cost_estimate=pl.CostEstimate(flops=flops, bytes_accessed=moved, transcendentals=0),
@@ -206,7 +252,7 @@
             jax.ShapeDtypeStruct((2 * STRIP + 16, HALF), F32),
         ),
         in_specs=[HBM] * 7,
-        out_specs=(VMEM, VMEM),
+        out_specs=(HBM, HBM),
         scratch_shapes=[
             pltpu.VMEM((2, HALF, STRIP), BF16),
             pltpu.VMEM((1, HALF), F32),
@@ -214,14 +260,29 @@
             pltpu.SMEM((16,), jnp.int32),
             pltpu.SMEM((32,), jnp.int32),
             pltpu.SMEM((16, 32), jnp.int32),
+            pltpu.VMEM((2 * STRIP, HALF), BF16),
+            pltpu.VMEM((2 * STRIP + 16, HALF), F32),
             pltpu.SemaphoreType.DMA((7,)),
+            pltpu.SemaphoreType.DMA((2,)),
         ],
         compiler_params=pltpu.CompilerParams(vmem_limit_bytes=60 * 1024 * 1024),
         cost_estimate=pl.CostEstimate(flops=0, bytes_accessed=1 << 20, transcendentals=0),
     )(*operands)
 
 
-SPREAD = [[16 * xl + 4 * n + (s + n) % 4 for n in range(4)] for xl in range(2) for s in range(4)]
+def groups():
+    gather = [
+        [32 * core + 16 * xl + (4 * n + 2 * core + j) % 16 for xl in range(2) for j in range(4)]
+        for core in range(2)
+        for n in range(4)
+    ]
+    reduce = [
+        [32 * core + 16 * xl + (4 * n + 2 * core + (s + n) % 4) % 16 for n in range(4)]
+        for core in range(2)
+        for xl in range(2)
+        for s in range(4)
+    ]
+    return gather, reduce
 
 
 def on_device(
@@ -241,32 +302,52 @@
     encode = call(
         encode_kernel, [VMEM], (8, 2 * STRIP, 2 * HALF), BF16, turned_scratch, moved=3 << 20
     )(pack)
-    shares = call(strip_kernel, [VMEM] * 3, (8, STRIP, 2 * STRIP), BF16, flops=1 << 29)(
-        own, other, encode
-    )
+    blocks = (8, STRIP, 2 * STRIP)
+    eight = pltpu.SemaphoreType.DMA((8,))
+    shares = call(
+        strip_kernel,
+        [VMEM] * 3,
+        blocks,
+        BF16,
+        [pltpu.VMEM(blocks, BF16), eight],
+        flops=1 << 29,
+        out=HBM,
+    )(own, other, encode)
 
     def decode(xl, pack):
         kernel = functools.partial(decode_kernel, xl)
         shape = (4, 2 * STRIP, 2 * HALF)
         return call(kernel, [VMEM], shape, BF16, turned_scratch, moved=2 << 20)(pack)
 
+    gather, reduce = groups()
+    line = ("core",) + FAC
     shares, pack = lax.optimization_barrier((shares, pack))
     low = decode(0, pack)
     shares, low = lax.optimization_barrier((lax.all_to_all(shares, ("xh", "y"), 0, 0), low))
-    strip = call(sum_kernel, [VMEM], (8, STRIP, 2 * STRIP), BF16)(shares)
+    strip = call(
+        sum_kernel, [VMEM], blocks, BF16, [pltpu.VMEM(blocks[1:], BF16), eight], out=HBM
+    )(shares)
     strip, pack = lax.optimization_barrier((strip, pack))
     high = decode(1, pack)
-    strips = lax.all_to_all(strip, ("xl", "zl"), 0, 0)
-    partial = call(subgrid_kernel, [VMEM] * 3, (4, 2 * STRIP, STRIP), BF16, flops=1 << 29)(
-        strips, low, high
-    )
-    received = lax.all_to_all(partial, FAC, 0, 0, axis_index_groups=SPREAD)
+    strips = lax.all_to_all(strip, line, 0, 0, axis_index_groups=gather)
+    quarters = (4, 2 * STRIP, STRIP)
+    partial = call(
+        subgrid_kernel,
+        [VMEM] * 3,
+        quarters,
+        BF16,
+        [pltpu.VMEM(quarters, BF16), pltpu.SemaphoreType.DMA((4,))],
+        flops=1 << 29,
+        out=HBM,
+    )(strips, low, high)
+    received = lax.all_to_all(partial, line, 0, 0, axis_index_groups=reduce)
     subgrid = call(
         place_kernel,
         [SMEM, VMEM],
         (2, SUBGRID, STRIP),
         F32,
-        [pltpu.VMEM((2, SUBGRID + STRIP, STRIP), F32)],
+        [pltpu.VMEM((2, SUBGRID + STRIP, STRIP), F32), pltpu.SemaphoreType.DMA((2,))],
+        out=HBM,
     )(column_place, received)
     return subgrid.reshape(1, 1, 2, SUBGRID, STRIP)
 

time: 76.6 us -> 74.5 us (0.973)
  the two profiles are of different devices: /device:TPU:70 before, /device:TPU:2 now
where the time goes in v2:
time: 74.5 us; the launch traced here: 74 us
  waiting for transfers between devices  39.8 us (53%)
  starting transfers between devices  24.3 us (33%)
  Pallas kernels  8.06 us (11%)
  local copies, waits for them, and re-layouts  1.17 us (2%)
    all_to_all x1, waiting for transfers between devices, on_device(): received = lax.all_to_all(partial, line, 0, 0, axis_index_groups=reduce)  16.8 us
    all_to_all x1, waiting for transfers between devices, on_device(): strips = lax.all_to_all(strip, line, 0, 0, axis_index_groups=gather)  11.8 us
    all_to_all x1, waiting for transfers between devices, on_device(): lax.all_to_all(shares, ('xh', 'y'), 0, 0)  11.1 us
    all_to_all x1, starting transfers between devices, on_device(): received = lax.all_to_all(partial, line, 0, 0, axis_index_groups=reduce)  8.98 us
    all_to_all x1, starting transfers between devices, on_device(): strips = lax.all_to_all(strip, line, 0, 0, axis_index_groups=gather)  7.37 us
    all_to_all x1, starting transfers between devices, on_device(): lax.all_to_all(shares, ('xh', 'y'), 0, 0)  6.04 us
    ppermute x1, starting transfers between devices, on_device(): other = lax.ppermute(own, 'core', [(0, 1), (1, 0)])  1.92 us
    pallas_call x1, Pallas kernels, prepare(): pl.pallas_call(prepare_kernel, out_shape=(jax.ShapeDtypeStruct((2 * STRIP...  1.89 us
  transfers between devices with their start and end apart: 4, of which 3 were waited for; matrix products, arithmetic and copies ran while one was open for 0% of the time, Pallas kernels for 2%

profile of v2, /device:TPU:2, one launch (start us, length us, event | category | flops | bytes accessed | tf_op | source)
XLA Modules:
  0.0 74.0 jit_solution(6813550530614519309)
XLA Ops:
  0.0 1.9 %shard_map.82 = (bf16[256,256]{1,0:T(8,128)(2,1)}, f32[272,256]{1,0:T(8,128)}) custom-call(bf16[2,256,128]{2,1,0:T(8,128)(2,1)} %facets_hbm.1, f32[1,256]{1,0:T(1,128)} %bitcast.4, f32[32,128]{1,0:T(8,128)} %bitcast.3, s32[16]{0:T(128)} %row_offset_hbm.1, s32[32]{0:T(128)} %offset_hbm.1, s32[16,32]{1,0:T(8,128)} %slot_hbm.1, f32[256,256]{1,0:T(8,128)} %constant.2.clone.base_hbm), custom_call_target="tpu_custom_call" | custom-call | bytes 1048576 | tf_op jit(solution)/shard_map/pallas_call | solution.py:248
  1.9 1.9 %collective-permute-start = (bf16[256,256]{1,0:T(8,128)(2,1)}, bf16[256,256]{1,0:T(8,128)(2,1)S(1)}, u32[]{:S(2)}, u32[]{:S(2)}) collective-permute-start(bf16[256,256]{1,0:T(8,128)(2,1)} %get-tuple-element.13.own_ref), channel_id=1, source_target_pairs={{0,32},{32,0},{1,33},{33,1},{2,34},{34,2},{3,35},{35,3},{4,36},{36... | collective-permute-start | bytes 393224 | tf_op jit(solution)/shard_map/ppermute | solution.py:301
  3.8 0.0 copy-start
  3.8 0.9 %copy-done = f32[272,256]{1,0:T(8,128)S(1)} copy-done((f32[272,256]{1,0:T(8,128)S(1)}, f32[272,256]{1,0:T(8,128)}, u32[]{:S(2)}) %copy-start) | copy-done | bytes 278552
  4.8 0.0 copy-start.2
  4.8 0.7 shard_map.83.table_ref
  5.5 0.0 copy-start.1
  5.5 0.0 collective-permute-done.other_ref
  5.5 0.2 copy-done.2
  5.7 1.5 %shard_map.84 = bf16[8,128,256]{2,1,0:T(8,128)(2,1)} custom-call(bf16[256,256]{1,0:T(8,128)(2,1)S(1)} %copy-done.2, bf16[256,256]{1,0:T(8,128)(2,1)S(1)} %collective-permute-done.other_ref, bf16[8,256,512]{2,1,0:T(8,128)(2,1)S(1)} %shard_map.83.table_ref), custom_call_target="tpu_custom_call" | custom-call | flops 536870912 | bytes 1048576 | tf_op jit(solution)/shard_map/pallas_call | solution.py:307
  7.2 6.0 %all-to-all-start = ((bf16[8,128,256]{2,1,0:T(8,128)(2,1)}), bf16[8,128,256]{2,1,0:T(8,128)(2,1)S(1)}, u32[]{:S(2)}, u32[]{:S(2)}) async-start(bf16[8,128,256]{2,1,0:T(8,128)(2,1)} %shard_map.84), calls=%async_computation | async-start | bytes 1048576 | tf_op jit(solution)/shard_map/all_to_all | solution.py:326
  13.2 0.0 copy-done.1
  13.2 0.4 shard_map.85.low_ref
  13.7 11.1 %all-to-all-done.parts_ref = bf16[8,128,256]{2,1,0:T(8,128)(2,1)S(1)} async-done(((bf16[8,128,256]{2,1,0:T(8,128)(2,1)}), bf16[8,128,256]{2,1,0:T(8,128)(2,1)S(1)}, u32[]{:S(2)}, u32[]{:S(2)}) %all-to-all-start) | async-done | bytes 524320 | tf_op jit(solution)/shard_map/all_to_all | solution.py:326
  24.8 0.9 %shard_map.86 = bf16[8,128,256]{2,1,0:T(8,128)(2,1)} custom-call(bf16[8,128,256]{2,1,0:T(8,128)(2,1)S(1)} %all-to-all-done.parts_ref), custom_call_target="tpu_custom_call" | custom-call | bytes 1048576 | tf_op jit(solution)/shard_map/pallas_call | solution.py:327
  25.7 7.4 %all-to-all-start.1 = ((bf16[8,128,256]{2,1,0:T(8,128)(2,1)}), bf16[8,128,256]{2,1,0:T(8,128)(2,1)S(1)}, u32[]{:S(2)}, u32[]{:S(2)}) async-start(bf16[8,128,256]{2,1,0:T(8,128)(2,1)} %shard_map.86), calls=%async_computation.1 | async-start | bytes 1048576 | tf_op jit(solution)/shard_map/all_to_all | solution.py:332
  33.1 0.4 shard_map.87.high_ref
  33.5 11.8 %all-to-all-done.1.strip_ref = bf16[8,128,256]{2,1,0:T(8,128)(2,1)S(1)} async-done(((bf16[8,128,256]{2,1,0:T(8,128)(2,1)}), bf16[8,128,256]{2,1,0:T(8,128)(2,1)S(1)}, u32[]{:S(2)}, u32[]{:S(2)}) %all-to-all-start.1) | async-done | bytes 524320 | tf_op jit(solution)/shard_map/all_to_all | solution.py:332
  45.3 1.4 %shard_map.88 = bf16[4,256,128]{2,1,0:T(8,128)(2,1)} custom-call(bf16[8,128,256]{2,1,0:T(8,128)(2,1)S(1)} %all-to-all-done.1.strip_ref, bf16[4,256,512]{2,1,0:T(8,128)(2,1)S(1)} %shard_map.85.low_ref, bf16[4,256,512]{2,1,0:T(8,128)(2,1)S(1)} %shard_map.87.high_ref), custom_call_target="tpu_custom_call" | custom-call | flops 536870912 | bytes 1048576 | tf_op jit(solution)/shard_map/pallas_call | solution.py:334
  46.8 9.0 %all-to-all-start.2 = ((bf16[4,256,128]{2,1,0:T(8,128)(2,1)}), bf16[4,256,128]{2,1,0:T(8,128)(2,1)S(1)}, u32[]{:S(2)}, u32[]{:S(2)}) async-start(bf16[4,256,128]{2,1,0:T(8,128)(2,1)} %shard_map.88), calls=%async_computation.2 | async-start | bytes 524288 | tf_op jit(solution)/shard_map/all_to_all | solution.py:343
  56.4 16.8 %all-to-all-done.2.parts_ref = bf16[4,256,128]{2,1,0:T(8,128)(2,1)S(1)} async-done(((bf16[4,256,128]{2,1,0:T(8,128)(2,1)}), bf16[4,256,128]{2,1,0:T(8,128)(2,1)S(1)}, u32[]{:S(2)}, u32[]{:S(2)}) %all-to-all-start.2) | async-done | bytes 262176 | tf_op jit(solution)/shard_map/all_to_all | solution.py:343
  73.2 0.9 %shard_map.89 = f32[2,512,128]{2,1,0:T(8,128)} custom-call(s32[1]{0:T(128)S(6)} %copy.9.place_ref, bf16[4,256,128]{2,1,0:T(8,128)(2,1)S(1)} %all-to-all-done.2.parts_ref), custom_call_target="tpu_custom_call" | custom-call | bytes 1048576 | tf_op jit(solution)/shard_map/pallas_call | solution.py:344
Async XLA Ops:
  1.9 3.6 %collective-permute-start = (bf16[256,256]{1,0:T(8,128)(2,1)}, bf16[256,256]{1,0:T(8,128)(2,1)S(1)}, u32[]{:S(2)}, u32[]{:S(2)}) collective-permute-start(bf16[256,256]{1,0:T(8,128)(2,1)} %get-tuple-element.13.own_ref), channel_id=1, source_target_pairs={{0,32},{32,0},{1,33},{33,1},{2,34},{34,2},{3,35},{35,3},{4,36},{36... | collective-permute-start | bytes 393224 | tf_op jit(solution)/shard_map/ppermute | solution.py:301
  3.8 1.0 %copy-start = (f32[272,256]{1,0:T(8,128)S(1)}, f32[272,256]{1,0:T(8,128)}, u32[]{:S(2)}) copy-start(f32[272,256]{1,0:T(8,128)} %get-tuple-element.20.pack_ref) | copy-start | bytes 835588
  4.8 0.9 %copy-start.2 = (bf16[256,256]{1,0:T(8,128)(2,1)S(1)}, bf16[256,256]{1,0:T(8,128)(2,1)}, u32[]{:S(2)}) copy-start(bf16[256,256]{1,0:T(8,128)(2,1)} %get-tuple-element.13.own_ref) | copy-start | bytes 393220
  5.5 7.8 %copy-start.1 = (f32[272,256]{1,0:T(8,128)S(1)}, f32[272,256]{1,0:T(8,128)}, u32[]{:S(2)}) copy-start(f32[272,256]{1,0:T(8,128)} %get-tuple-element.20.pack_ref) | copy-start | bytes 835588
  7.2 17.6 %all-to-all-start = ((bf16[8,128,256]{2,1,0:T(8,128)(2,1)}), bf16[8,128,256]{2,1,0:T(8,128)(2,1)S(1)}, u32[]{:S(2)}, u32[]{:S(2)}) async-start(bf16[8,128,256]{2,1,0:T(8,128)(2,1)} %shard_map.84), calls=%async_computation | async-start | bytes 1048576 | tf_op jit(solution)/shard_map/all_to_all | solution.py:326
  25.7 19.6 %all-to-all-start.1 = ((bf16[8,128,256]{2,1,0:T(8,128)(2,1)}), bf16[8,128,256]{2,1,0:T(8,128)(2,1)S(1)}, u32[]{:S(2)}, u32[]{:S(2)}) async-start(bf16[8,128,256]{2,1,0:T(8,128)(2,1)} %shard_map.86), calls=%async_computation.1 | async-start | bytes 1048576 | tf_op jit(solution)/shard_map/all_to_all | solution.py:332
  46.8 26.4 %all-to-all-start.2 = ((bf16[4,256,128]{2,1,0:T(8,128)(2,1)}), bf16[4,256,128]{2,1,0:T(8,128)(2,1)S(1)}, u32[]{:S(2)}, u32[]{:S(2)}) async-start(bf16[4,256,128]{2,1,0:T(8,128)(2,1)} %shard_map.88), calls=%async_computation.2 | async-start | bytes 524288 | tf_op jit(solution)/shard_map/all_to_all | solution.py:343

commit v3 on v2

--- a/solution.py
+++ b/solution.py
@@ -1,4 +1,3 @@
-import functools
 import math
 
 import jax
@@ -17,6 +16,10 @@
 SIZES = (2, 4, 2, 2, 4, 4)
 COL = SPLIT[:3]
 FAC = SPLIT[3:]
+PLANE = (0, 1, 2, 3, 4, 5, 6, 7)
+RUN = (0, 1, 2, 3, 4, 5, 6, 7)
+RUNS = ((3, 2, 1, 0), (3, 2, 1, 0))
+TWIST = (0, 1, 2, 3)
 F32 = jnp.float32
 BF16 = jnp.bfloat16
 VMEM = pl.BlockSpec(memory_space=pltpu.VMEM)
@@ -133,18 +136,14 @@
     own_copy.start()
     for copy in copies[3:6]:
         copy.wait()
-    pack_ref[ENCODE] = spread([row_offset_ref[2 * n + core] for n in range(8)])
-    pack_ref[DECODE] = spread(
-        [
-            offset_ref[
-                slot_ref[
-                    2 * pair + core, 16 * xl + ((4 * n + 2 * core + ((step - line + n) & 3)) & 15)
-                ]
-                & 31
-            ]
-            for n in range(4)
-        ]
-    )
+    pack_ref[ENCODE] = spread([row_offset_ref[2 * n + core] for n in PLANE])
+    slots = []
+    twist = sum(jnp.where(line == n, TWIST[n], 0) for n in range(4))
+    for first, second in zip(*RUNS):
+        run = jnp.where(core == 0, first, second)
+        away = jnp.where(core == 0, TWIST[first], TWIST[second])
+        slots.append(16 * xl + ((4 * run + 2 * core + ((step - twist + away) & 3)) & 15))
+    pack_ref[DECODE] = spread([offset_ref[slot_ref[2 * pair + core, slot] & 31] for slot in slots])
     copies[6].wait()
     pack_copy = pltpu.make_async_copy(pack_ref, pack_hbm, out_sems.at[1])
     pack_copy.start()
@@ -158,20 +157,14 @@
     fill_tables(pack_ref, ENCODE, 8, [2 * pair + core, 2 * pair + 1 - core], out_ref, turned_ref)
 
 
-def decode_kernel(xl, pack_ref, out_ref, turned_ref):
+def decode_kernel(place_ref, pack_ref, out_ref, spot_ref, turned_ref):
+    spot_ref[...] = jnp.full((8, STRIP), place_ref[0], jnp.int32)
     core, _, line, _ = position()
-    blocks = [8 * xl + ((2 * line + core + half) & 7) for half in range(2)]
+    blocks = [8 * xl + ((2 * line + core + half) & 7) for xl in range(2) for half in range(2)]
     fill_tables(pack_ref, DECODE, 4, blocks, out_ref, turned_ref)
 
 
-def sent(n, out_ref, out_hbm, sems):
-    copy = pltpu.make_async_copy(out_ref.at[n], out_hbm.at[n], sems.at[n])
-    copy.start()
-    return copy
-
-
-def strip_kernel(own_ref, other_ref, table_ref, out_hbm, out_ref, sems):
-    copies = []
+def strip_kernel(own_ref, other_ref, table_ref, out_ref):
     for n in range(8):
         product = lax.dot_general(
             own_ref[...], table_ref[n, :, :HALF], NT, preferred_element_type=F32
@@ -180,9 +173,6 @@
         )
         out_ref[n, :, :STRIP] = (product[:STRIP, :STRIP] - product[STRIP:, STRIP:]).astype(BF16)
         out_ref[n, :, STRIP:] = (product[:STRIP, STRIP:] + product[STRIP:, :STRIP]).astype(BF16)
-        copies.append(sent(n, out_ref, out_hbm, sems))
-    for copy in copies:
-        copy.wait()
 
 
 def sum_kernel(parts_ref, out_hbm, total_ref, sems):
@@ -197,23 +187,16 @@
         copy.wait()
 
 
-def subgrid_kernel(strip_ref, low_ref, high_ref, out_hbm, out_ref, sems):
-    low = strip_ref[:4].reshape(4 * STRIP, 2 * STRIP)
-    high = strip_ref[4:].reshape(4 * STRIP, 2 * STRIP)
-    copies = []
+def subgrid_kernel(strip_ref, table_ref, out_ref):
+    strip = jnp.concatenate([strip_ref[RUN.index(n)] for n in range(8)])
     for n in range(4):
-        product = jnp.dot(low_ref[n], low, preferred_element_type=F32) + jnp.dot(
-            high_ref[n], high, preferred_element_type=F32
-        )
+        product = jnp.dot(table_ref[n], strip, preferred_element_type=F32)
         out_ref[n, :STRIP] = (product[:STRIP, :STRIP] - product[STRIP:, STRIP:]).astype(BF16)
         out_ref[n, STRIP:] = (product[:STRIP, STRIP:] + product[STRIP:, :STRIP]).astype(BF16)
-        copies.append(sent(n, out_ref, out_hbm, sems))
-    for copy in copies:
-        copy.wait()
 
 
 def place_kernel(place_ref, parts_ref, out_hbm, scratch_ref, sems):
-    place = place_ref[0] & (SUBGRID - 1)
+    place = jnp.max(place_ref[...]) & (SUBGRID - 1)
     scratch_ref[...] = jnp.zeros_like(scratch_ref)
     copies = []
     for part in range(2):
@@ -233,9 +216,13 @@
 
 
 def call(kernel, specs, shape, dtype, scratch=(), flops=0, moved=1 << 20, out=VMEM):
+    if isinstance(shape, list):
+        result = [jax.ShapeDtypeStruct(*pair) for pair in zip(shape, dtype)]
+    else:
+        result = jax.ShapeDtypeStruct(shape, dtype)
     return pl.pallas_call(
         kernel,
-        out_shape=jax.ShapeDtypeStruct(shape, dtype),
+        out_shape=result,
         in_specs=specs,
         out_specs=out,
         scratch_shapes=list(scratch),
@@ -272,12 +259,12 @@
 
 def groups():
     gather = [
-        [32 * core + 16 * xl + (4 * n + 2 * core + j) % 16 for xl in range(2) for j in range(4)]
+        [32 * core + 16 * (j // 4) + (4 * n + 2 * core + j % 4) % 16 for j in RUN]
         for core in range(2)
         for n in range(4)
     ]
     reduce = [
-        [32 * core + 16 * xl + (4 * n + 2 * core + (s + n) % 4) % 16 for n in range(4)]
+        [32 * core + 16 * xl + (4 * n + 2 * core + (s + TWIST[n]) % 4) % 16 for n in RUNS[core]]
         for core in range(2)
         for xl in range(2)
         for s in range(4)
@@ -303,52 +290,46 @@
         encode_kernel, [VMEM], (8, 2 * STRIP, 2 * HALF), BF16, turned_scratch, moved=3 << 20
     )(pack)
     blocks = (8, STRIP, 2 * STRIP)
-    eight = pltpu.SemaphoreType.DMA((8,))
-    shares = call(
-        strip_kernel,
-        [VMEM] * 3,
+    shares = call(strip_kernel, [VMEM] * 3, blocks, BF16, flops=1 << 29)(own, other, encode)
+    gather, reduce = groups()
+    line = ("core",) + FAC
+    shares = lax.all_to_all(shares, ("xh", "y"), 0, 0, axis_index_groups=[list(PLANE)])
+    strip = call(
+        sum_kernel,
+        [VMEM],
         blocks,
         BF16,
-        [pltpu.VMEM(blocks, BF16), eight],
-        flops=1 << 29,
+        [pltpu.VMEM(blocks[1:], BF16), pltpu.SemaphoreType.DMA((8,))],
         out=HBM,
-    )(own, other, encode)
-
-    def decode(xl, pack):
-        kernel = functools.partial(decode_kernel, xl)
-        shape = (4, 2 * STRIP, 2 * HALF)
-        return call(kernel, [VMEM], shape, BF16, turned_scratch, moved=2 << 20)(pack)
-
-    gather, reduce = groups()
-    line = ("core",) + FAC
-    shares, pack = lax.optimization_barrier((shares, pack))
-    low = decode(0, pack)
-    shares, low = lax.optimization_barrier((lax.all_to_all(shares, ("xh", "y"), 0, 0), low))
-    strip = call(
-        sum_kernel, [VMEM], blocks, BF16, [pltpu.VMEM(blocks[1:], BF16), eight], out=HBM
     )(shares)
     strip, pack = lax.optimization_barrier((strip, pack))
-    high = decode(1, pack)
+    decode, spot = call(
+        decode_kernel,
+        [SMEM, VMEM],
+        [(4, 2 * STRIP, 4 * HALF), (8, STRIP)],
+        [BF16, jnp.int32],
+        turned_scratch,
+        moved=3 << 20,
+        out=[VMEM, VMEM],
+    )(column_place, pack)
     strips = lax.all_to_all(strip, line, 0, 0, axis_index_groups=gather)
     quarters = (4, 2 * STRIP, STRIP)
     partial = call(
         subgrid_kernel,
-        [VMEM] * 3,
+        [VMEM] * 2,
         quarters,
         BF16,
-        [pltpu.VMEM(quarters, BF16), pltpu.SemaphoreType.DMA((4,))],
         flops=1 << 29,
-        out=HBM,
-    )(strips, low, high)
+    )(strips, decode)
     received = lax.all_to_all(partial, line, 0, 0, axis_index_groups=reduce)
     subgrid = call(
         place_kernel,
-        [SMEM, VMEM],
+        [VMEM, VMEM],
         (2, SUBGRID, STRIP),
         F32,
         [pltpu.VMEM((2, SUBGRID + STRIP, STRIP), F32), pltpu.SemaphoreType.DMA((2,))],
         out=HBM,
-    )(column_place, received)
+    )(spot, received)
     return subgrid.reshape(1, 1, 2, SUBGRID, STRIP)
 
 

time: 74.5 us -> 72.8 us (0.977)
  the two profiles are of different devices: /device:TPU:2 before, /device:TPU:64 now
where the time goes in v3:
time: 72.8 us; the launch traced here: 72.4 us
  blocking collectives  49.2 us (68%)
  starting transfers between devices  7.51 us (10%)
  waiting for transfers between devices  6.98 us (10%)
  Pallas kernels  6.79 us (9%)
  local copies, waits for them, and re-layouts  1.18 us (2%)
  between operations  0.74 us (1%)
    all_to_all x1, blocking collectives, on_device(): received = lax.all_to_all(partial, line, 0, 0, axis_index_groups=reduce)  30.3 us
    all_to_all x1, blocking collectives, on_device(): lax.all_to_all(shares, ('xh', 'y'), 0, 0, axis_index_groups=[list(PLANE)])  18.9 us
    all_to_all x1, waiting for transfers between devices, on_device(): strips = lax.all_to_all(strip, line, 0, 0, axis_index_groups=gather)  6.98 us
    all_to_all x1, starting transfers between devices, on_device(): strips = lax.all_to_all(strip, line, 0, 0, axis_index_groups=gather)  5.59 us
    ppermute x1, starting transfers between devices, on_device(): other = lax.ppermute(own, 'core', [(0, 1), (1, 0)])  1.92 us
    pallas_call x1, Pallas kernels, prepare(): pl.pallas_call(prepare_kernel, out_shape=(jax.ShapeDtypeStruct((2 * STRIP...  1.88 us
  transfers between devices with their start and end apart: 2, of which 1 were waited for; matrix products, arithmetic and copies ran while one was open for 0% of the time, Pallas kernels for 2%

profile of v3, /device:TPU:64, one launch (start us, length us, event | category | flops | bytes accessed | tf_op | source)
XLA Modules:
  0.0 72.4 jit_solution(10600057614045343828)
XLA Ops:
  0.0 1.9 %shard_map.82 = (bf16[256,256]{1,0:T(8,128)(2,1)}, f32[272,256]{1,0:T(8,128)}) custom-call(bf16[2,256,128]{2,1,0:T(8,128)(2,1)} %facets_hbm.1, f32[1,256]{1,0:T(1,128)} %bitcast.4, f32[32,128]{1,0:T(8,128)} %bitcast.3, s32[16]{0:T(128)} %row_offset_hbm.1, s32[32]{0:T(128)} %offset_hbm.1, s32[16,32]{1,0:T(8,128)} %slot_hbm.1, f32[256,256]{1,0:T(8,128)} %constant.2.clone.base_hbm), custom_call_target="tpu_custom_call" | custom-call | bytes 1048576 | tf_op jit(solution)/shard_map/pallas_call | solution.py:235
  1.9 1.9 %collective-permute-start = (bf16[256,256]{1,0:T(8,128)(2,1)}, bf16[256,256]{1,0:T(8,128)(2,1)S(1)}, u32[]{:S(2)}, u32[]{:S(2)}) collective-permute-start(bf16[256,256]{1,0:T(8,128)(2,1)} %get-tuple-element.11.own_ref), channel_id=1, source_target_pairs={{0,32},{32,0},{1,33},{33,1},{2,34},{34,2},{3,35},{35,3},{4,36},{36... | collective-permute-start | bytes 393224 | tf_op jit(solution)/shard_map/ppermute | solution.py:288
  3.8 0.0 copy-start
  3.8 0.9 %copy-done = f32[272,256]{1,0:T(8,128)S(1)} copy-done((f32[272,256]{1,0:T(8,128)S(1)}, f32[272,256]{1,0:T(8,128)}, u32[]{:S(2)}) %copy-start) | copy-done | bytes 278552
  4.8 0.0 copy-start.2
  4.8 0.7 shard_map.83.table_ref
  5.4 0.0 collective-permute-done.other_ref
  5.5 0.2 copy-done.2
  5.7 0.7 %shard_map.84 = bf16[8,128,256]{2,1,0:T(8,128)(2,1)S(1)} custom-call(bf16[256,256]{1,0:T(8,128)(2,1)S(1)} %copy-done.2, bf16[256,256]{1,0:T(8,128)(2,1)S(1)} %collective-permute-done.other_ref, bf16[8,256,512]{2,1,0:T(8,128)(2,1)S(1)} %shard_map.83.table_ref), custom_call_target="tpu_custom_call" | custom-call | flops 536870912 | bytes 1048576 | tf_op jit(solution)/shard_map/pallas_call | solution.py:293
  6.4 0.0 copy-start.1
  6.4 18.9 %all_to_all.15.parts_ref = bf16[8,128,256]{2,1,0:T(8,128)(2,1)S(1)} all-to-all(bf16[8,128,256]{2,1,0:T(8,128)(2,1)S(1)} %shard_map.84), channel_id=1, replica_groups={{0,64,128,192,256,320,384,448},{1,65,129,193,257,321,385,449},{2,66,130..., dimensions={0} | all-to-all | bytes 1048576 | tf_op jit(solution)/shard_map/all_to_all | solution.py:296
  25.3 0.9 %shard_map.85 = bf16[8,128,256]{2,1,0:T(8,128)(2,1)} custom-call(bf16[8,128,256]{2,1,0:T(8,128)(2,1)S(1)} %all_to_all.15.parts_ref), custom_call_target="tpu_custom_call" | custom-call | bytes 1048576 | tf_op jit(solution)/shard_map/pallas_call | solution.py:297
  26.3 5.6 %all-to-all-start.1 = ((bf16[8,128,256]{2,1,0:T(8,128)(2,1)}), bf16[8,128,256]{2,1,0:T(8,128)(2,1)S(1)}, u32[]{:S(2)}, u32[]{:S(2)}) async-start(bf16[8,128,256]{2,1,0:T(8,128)(2,1)} %shard_map.85), calls=%async_computation.1 | async-start | bytes 1048576 | tf_op jit(solution)/shard_map/all_to_all | solution.py:315
  32.5 0.0 copy-done.1
  32.5 0.9 %shard_map.86 = (bf16[4,256,1024]{2,1,0:T(8,128)(2,1)S(1)}, s32[8,128]{1,0:T(8,128)S(1)}) custom-call(s32[1]{0:T(128)S(6)} %copy.9.place_ref, f32[272,256]{1,0:T(8,128)S(1)} %copy-done.1), custom_call_target="tpu_custom_call" | custom-call | bytes 3145728 | tf_op jit(solution)/shard_map/pallas_call | solution.py:306
  33.4 7.0 %all-to-all-done.1.strip_ref = bf16[8,128,256]{2,1,0:T(8,128)(2,1)S(1)} async-done(((bf16[8,128,256]{2,1,0:T(8,128)(2,1)}), bf16[8,128,256]{2,1,0:T(8,128)(2,1)S(1)}, u32[]{:S(2)}, u32[]{:S(2)}) %all-to-all-start.1) | async-done | bytes 524320 | tf_op jit(solution)/shard_map/all_to_all | solution.py:315
  40.4 0.7 shard_map.87
  41.1 30.3 %all_to_all.16.parts_ref = bf16[4,256,128]{2,1,0:T(8,128)(2,1)S(1)} all-to-all(bf16[4,256,128]{2,1,0:T(8,128)(2,1)S(1)} %shard_map.87), channel_id=1, replica_groups={{15,10,5,0},{12,11,6,1},{13,8,7,2},{14,9,4,3},{31,26,21,16},{28,27,22,1..., dimensions={0} | all-to-all | bytes 524288 | tf_op jit(solution)/shard_map/all_to_all | solution.py:324
  71.4 1.0 %shard_map.88 = f32[2,512,128]{2,1,0:T(8,128)} custom-call(s32[8,128]{1,0:T(8,128)S(1)} %get-tuple-element.14.place_ref, bf16[4,256,128]{2,1,0:T(8,128)(2,1)S(1)} %all_to_all.16.parts_ref), custom_call_target="tpu_custom_call" | custom-call | bytes 1048576 | tf_op jit(solution)/shard_map/pallas_call | solution.py:325
Async XLA Ops:
  1.9 3.6 %collective-permute-start = (bf16[256,256]{1,0:T(8,128)(2,1)}, bf16[256,256]{1,0:T(8,128)(2,1)S(1)}, u32[]{:S(2)}, u32[]{:S(2)}) collective-permute-start(bf16[256,256]{1,0:T(8,128)(2,1)} %get-tuple-element.11.own_ref), channel_id=1, source_target_pairs={{0,32},{32,0},{1,33},{33,1},{2,34},{34,2},{3,35},{35,3},{4,36},{36... | collective-permute-start | bytes 393224 | tf_op jit(solution)/shard_map/ppermute | solution.py:288
  3.8 1.0 %copy-start = (f32[272,256]{1,0:T(8,128)S(1)}, f32[272,256]{1,0:T(8,128)}, u32[]{:S(2)}) copy-start(f32[272,256]{1,0:T(8,128)} %get-tuple-element.13.pack_ref) | copy-start | bytes 835588
  4.8 0.9 %copy-start.2 = (bf16[256,256]{1,0:T(8,128)(2,1)S(1)}, bf16[256,256]{1,0:T(8,128)(2,1)}, u32[]{:S(2)}) copy-start(bf16[256,256]{1,0:T(8,128)(2,1)} %get-tuple-element.11.own_ref) | copy-start | bytes 393220
  6.4 26.1 %copy-start.1 = (f32[272,256]{1,0:T(8,128)S(1)}, f32[272,256]{1,0:T(8,128)}, u32[]{:S(2)}) copy-start(f32[272,256]{1,0:T(8,128)} %get-tuple-element.13.pack_ref) | copy-start | bytes 835588
  26.3 14.1 %all-to-all-start.1 = ((bf16[8,128,256]{2,1,0:T(8,128)(2,1)}), bf16[8,128,256]{2,1,0:T(8,128)(2,1)S(1)}, u32[]{:S(2)}, u32[]{:S(2)}) async-start(bf16[8,128,256]{2,1,0:T(8,128)(2,1)} %shard_map.85), calls=%async_computation.1 | async-start | bytes 1048576 | tf_op jit(solution)/shard_map/all_to_all | solution.py:315

commit v4 on v3

v4 whole, which is shorter than its diff:
```python
import math

import jax
import jax.numpy as jnp
import numpy as np
from jax import lax
from jax.experimental import pallas as pl
from jax.experimental.pallas import tpu as pltpu
from jax.sharding import Mesh, PartitionSpec as P

FACET = 4096
STRIP = 128
SUBGRID = 512
HALF = 256
SPLIT = ("xh", "y", "core", "xl", "zh", "zl")
SIZES = (2, 4, 2, 2, 4, 4)
COL = SPLIT[:3]
FAC = SPLIT[3:]
RUN = (0, 1, 2, 3)
RUNS = ((3, 2, 1, 0), (3, 2, 1, 0))
TWIST = (0, 1, 2, 3)
F32 = jnp.float32
BF16 = jnp.bfloat16
VMEM = pl.BlockSpec(memory_space=pltpu.VMEM)
HBM = pl.BlockSpec(memory_space=pltpu.HBM)
SMEM = pl.BlockSpec(memory_space=pltpu.SMEM)
BASE = 48
ENCODE = slice(BASE, BASE + 8)
DECODE = slice(BASE + 8, BASE + 16)
OWN = slice(BASE + 16, BASE + 16 + HALF)
AHEAD = 6
NT = (((1,), (1,)), ((), ()))


def base_table():
    def rows(ks, scale):
        angle = (ks[:, None] * np.arange(HALF)[None, :] % FACET) * (2.0 * math.pi / FACET)
        return [np.cos(angle) * scale, -np.sin(angle) * scale]

    small, large = np.arange(16), 16 * np.arange(8)
    return np.concatenate(rows(small, 1.0) + rows(large, 1.0 / math.sqrt(FACET))).astype(np.float32)


def unit(phase):
    angle = phase.astype(F32) * (2.0 * math.pi / FACET)
    return jnp.cos(angle), -jnp.sin(angle)


def turned(pack_ref, turned_ref, block):
    k = lax.broadcasted_iota(jnp.int32, (16, HALF), 0)
    real, imag = unit((k * block & 15) * HALF)
    base_real, base_imag = pack_ref[0:16, :], pack_ref[16:32, :]
    real, imag = base_real * real - base_imag * imag, base_real * imag + base_imag * real
    for large in range(8):
        row_real = pack_ref[32 + large : 33 + large, :]
        row_imag = pack_ref[40 + large : 41 + large, :]
        rows = pl.ds(16 * large, 16)
        turned_ref[0, rows, :] = row_real * real - row_imag * imag
        turned_ref[1, rows, :] = row_real * imag + row_imag * real


def position():
    core, xl, zh, zl = (lax.axis_index(name) for name in ("core", "xl", "zh", "zl"))
    place = (4 * zh + zl - 2 * core) & 15
    return core, xl, place >> 2, place & 3


def spread(starts):
    row = lax.broadcasted_iota(jnp.int32, (8, HALF), 0)
    first = jnp.zeros((8, HALF), jnp.int32)
    for n, start in enumerate(starts):
        first = jnp.where(row == n, start, first)
    return first.astype(F32)


def fill_tables(pack_ref, firsts, turn, blocks, outs, turned_ref):
    lane = lax.broadcasted_iota(jnp.int32, (8, HALF), 1)
    first = pack_ref[firsts].astype(jnp.int32)
    for c, block in enumerate(blocks):
        turned(pack_ref, turned_ref, block)
        real, imag = unit(first * (block * HALF + lane) & (FACET - 1))
        for k in range(0, STRIP, 16):
            rows = pl.ds(k, 16)
            base_real, base_imag = turned_ref[0, rows, :], turned_ref[1, rows, :]
            row = k // turn * 2 * turn + k % turn
            for n, out in outs.items():
                own_real, own_imag = real[n : n + 1], imag[n : n + 1]
                out[pl.ds(row, 16), HALF * c : HALF * (c + 1)] = (
                    own_real * base_real - own_imag * base_imag
                ).astype(BF16)
                out[pl.ds(row + turn, 16), HALF * c : HALF * (c + 1)] = (
                    own_real * base_imag + own_imag * base_real
                ).astype(BF16)


def prepare_kernel(
    facets_hbm,
    row_hbm,
    column_hbm,
    row_offset_hbm,
    offset_hbm,
    slot_hbm,
    base_hbm,
    out_hbm,
    first_hbm,
    pack_hbm,
    facets_ref,
    row_ref,
    column_ref,
    row_offset_ref,
    offset_ref,
    slot_ref,
    out_ref,
    pack_ref,
    sems,
    out_sems,
):
    core, xl, line, step = position()
    pair = lax.axis_index("xh") * 4 + lax.axis_index("y")
    fac = (xl * 4 + lax.axis_index("zh")) * 4 + lax.axis_index("zl")
    copies = [
        pltpu.make_async_copy(source, target, sems.at[n])
        for n, (source, target) in enumerate(
            [
                (facets_hbm, facets_ref),
                (row_hbm, row_ref),
                (column_hbm, column_ref),
                (row_offset_hbm, row_offset_ref),
                (offset_hbm, offset_ref),
                (slot_hbm, slot_ref),
                (base_hbm, pack_ref.at[pl.ds(0, BASE)]),
            ]
        )
    ]
    for copy in copies:
        copy.start()
    for copy in copies[:3]:
        copy.wait()
    column = column_ref[pl.ds(fac, 1), :]
    for part in range(2):
        scaled = facets_ref[part].astype(F32) * column
        block = (scaled.T * row_ref[...]).astype(BF16)
        out_ref[STRIP * part : STRIP * (part + 1), :] = block
        pack_ref[BASE + 16 + STRIP * part : BASE + 16 + STRIP * (part + 1), :] = block.astype(F32)
    own_copy = pltpu.make_async_copy(out_ref, out_hbm, out_sems.at[0])
    own_copy.start()
    for copy in copies[3:6]:
        copy.wait()
    pack_ref[ENCODE] = spread([row_offset_ref[2 * n + core] for n in range(8)])
    slots = []
    twist = sum(jnp.where(line == n, TWIST[n], 0) for n in range(4))
    for first, second in zip(*RUNS):
        run = jnp.where(core == 0, first, second)
        away = jnp.where(core == 0, TWIST[first], TWIST[second])
        slots.append((4 * run + 2 * core + ((step - twist + away) & 3)) & 15)
    slots += [slot + 16 for slot in slots]
    pack_ref[DECODE] = spread([offset_ref[slot_ref[2 * pair + core, slot] & 31] for slot in slots])
    copies[6].wait()
    first_copy = pltpu.make_async_copy(pack_ref, first_hbm, out_sems.at[1])
    first_copy.start()
    pack_copy = pltpu.make_async_copy(pack_ref.at[pl.ds(0, BASE + 16)], pack_hbm, out_sems.at[2])
    pack_copy.start()
    own_copy.wait()
    first_copy.wait()
    pack_copy.wait()


def encode_kernel(pack_ref, out_ref, turned_ref):
    core = lax.axis_index("core")
    pair = lax.axis_index("xh") * 4 + lax.axis_index("y")
    outs = {n: out_ref.at[n] for n in range(8)}
    blocks = [2 * pair + core, 2 * pair + 1 - core]
    fill_tables(pack_ref, ENCODE, STRIP // 2, blocks, outs, turned_ref)


def decode_tables(pack_ref, outs, turned_ref):
    core, _, line, _ = position()
    blocks = [8 * xl + ((2 * line + core + half) & 7) for xl in range(2) for half in range(2)]
    fill_tables(pack_ref, DECODE, STRIP, blocks, outs, turned_ref)


def decode_kernel(place_ref, pack_ref, out_ref, spot_ref, turned_ref):
    spot_ref[...] = jnp.full((8, STRIP), place_ref[0], jnp.int32)
    decode_tables(pack_ref, {n: out_ref.at[n] for n in range(AHEAD)}, turned_ref)


def joined(real_rows, imag_rows):
    lane = lax.broadcasted_iota(jnp.int32, real_rows.shape, 1)
    turned = pltpu.roll(imag_rows, STRIP // 2, 1)
    return real_rows + jnp.where(lane < STRIP // 2, -turned, turned)


def strip_kernel(first_ref, other_ref, table_ref, out_ref):
    own = first_ref[OWN].astype(BF16)
    for n in range(8):
        product = lax.dot_general(
            own, table_ref[n, :, :HALF], NT, preferred_element_type=F32
        ) + lax.dot_general(
            other_ref[...], table_ref[n, :, HALF:], NT, preferred_element_type=F32
        )
        for half in range(2):
            part = product[:, STRIP * half : STRIP * (half + 1)]
            out_ref[2 * n + half] = joined(part[:STRIP], part[STRIP:]).astype(BF16)


def sum_kernel(parts_ref, out_hbm, total_ref, sems):
    for xl in range(2):
        total = parts_ref[xl].astype(F32)
        for n in range(1, 8):
            total += parts_ref[2 * n + xl].astype(F32)
        total_ref[STRIP * xl : STRIP * (xl + 1), :] = total.astype(BF16)
    copies = [pltpu.make_async_copy(total_ref, out_hbm.at[n], sems.at[n]) for n in range(4)]
    for copy in copies:
        copy.start()
    for copy in copies:
        copy.wait()


def subgrid_kernel(strip_ref, ahead_ref, pack_ref, out_ref, late_ref, turned_ref):
    decode_tables(pack_ref, {n: late_ref.at[n - AHEAD] for n in range(AHEAD, 8)}, turned_ref)
    strip = jnp.concatenate(
        [
            strip_ref[RUN.index(n), STRIP * xl : STRIP * (xl + 1), :]
            for xl in range(2)
            for n in range(4)
        ]
    )
    for n in range(8):
        table = ahead_ref[n] if n < AHEAD else late_ref[n - AHEAD]
        product = jnp.dot(table, strip, preferred_element_type=F32)
        out_ref[n] = joined(product[:STRIP], product[STRIP:]).astype(BF16)


def place_kernel(place_ref, parts_ref, out_hbm, scratch_ref, sems):
    place = jnp.max(place_ref[...]) & (SUBGRID - 1)
    scratch_ref[...] = jnp.zeros_like(scratch_ref)
    halves = []
    for xl in range(2):
        total = parts_ref[4 * xl].astype(F32)
        for n in range(1, 4):
            total += parts_ref[4 * xl + n].astype(F32)
        halves.append(total)
    low = lax.broadcasted_iota(jnp.int32, (STRIP, STRIP), 1) < STRIP // 2
    copies = []
    for part in range(2):
        turned = pltpu.roll(halves[1 - part], STRIP // 2, 1)
        whole = jnp.where(low, turned, halves[1]) if part else jnp.where(low, halves[0], turned)
        scratch_ref[part, pl.ds(place, STRIP), :] = whole
        scratch_ref[part, :STRIP, :] += scratch_ref[part, SUBGRID:, :]
        copy = pltpu.make_async_copy(
            scratch_ref.at[part, pl.ds(0, SUBGRID)], out_hbm.at[part], sems.at[part]
        )
        copy.start()
        copies.append(copy)
    for copy in copies:
        copy.wait()


def call(kernel, specs, shape, dtype, scratch=(), flops=0, moved=1 << 20, out=VMEM):
    if isinstance(shape, list):
        result = [jax.ShapeDtypeStruct(*pair) for pair in zip(shape, dtype)]
    else:
        result = jax.ShapeDtypeStruct(shape, dtype)
    return pl.pallas_call(
        kernel,
        out_shape=result,
        in_specs=specs,
        out_specs=out,
        scratch_shapes=list(scratch),
        compiler_params=pltpu.CompilerParams(vmem_limit_bytes=24 * 1024 * 1024),
        cost_estimate=pl.CostEstimate(flops=flops, bytes_accessed=moved, transcendentals=0),
    )


def prepare(*operands):
    return pl.pallas_call(
        prepare_kernel,
        out_shape=(
            jax.ShapeDtypeStruct((2 * STRIP, HALF), BF16),
            jax.ShapeDtypeStruct((BASE + 16 + HALF, HALF), F32),
            jax.ShapeDtypeStruct((BASE + 16, HALF), F32),
        ),
        in_specs=[HBM] * 7,
        out_specs=(HBM, HBM, HBM),
        scratch_shapes=[
            pltpu.VMEM((2, HALF, STRIP), BF16),
            pltpu.VMEM((1, HALF), F32),
            pltpu.VMEM((32, STRIP), F32),
            pltpu.SMEM((16,), jnp.int32),
            pltpu.SMEM((32,), jnp.int32),
            pltpu.SMEM((16, 32), jnp.int32),
            pltpu.VMEM((2 * STRIP, HALF), BF16),
            pltpu.VMEM((BASE + 16 + HALF, HALF), F32),
            pltpu.SemaphoreType.DMA((7,)),
            pltpu.SemaphoreType.DMA((3,)),
        ],
        compiler_params=pltpu.CompilerParams(vmem_limit_bytes=60 * 1024 * 1024),
        cost_estimate=pl.CostEstimate(flops=0, bytes_accessed=1 << 20, transcendentals=0),
    )(*operands)


def groups():
    gather = [
        [32 * core + 16 * xl + (4 * n + 2 * core + j) % 16 for j in RUN]
        for core in range(2)
        for xl in range(2)
        for n in range(4)
    ]
    reduce = [
        [
            32 * core + 16 * xl + (4 * n + 2 * core + (s + TWIST[n]) % 4) % 16
            for xl in range(2)
            for n in RUNS[core]
        ]
        for core in range(2)
        for s in range(4)
    ]
    return gather, reduce


def on_device(
    facets, row_taper, column_taper, column_place, row_offset, column_offset, slot_subgrid
):
    turned_scratch = [pltpu.VMEM((2, STRIP, HALF), F32)]
    own, first, pack = prepare(
        facets,
        row_taper.reshape(1, HALF),
        column_taper.reshape(32, STRIP),
        row_offset,
        column_offset,
        slot_subgrid,
        jnp.asarray(base_table()),
    )
    other = lax.ppermute(own, "core", [(0, 1), (1, 0)])
    encode = call(
        encode_kernel, [VMEM], (8, 2 * STRIP, 2 * HALF), BF16, turned_scratch, moved=3 << 20
    )(first)
    shares = call(strip_kernel, [VMEM] * 3, (16, STRIP, STRIP), BF16, flops=1 << 29)(
        first, other, encode
    )
    gather, reduce = groups()
    line = ("core",) + FAC
    shares = lax.all_to_all(shares, ("xh", "y", "xl"), 0, 0)
    strip = call(
        sum_kernel,
        [VMEM],
        (4, 2 * STRIP, STRIP),
        BF16,
        [pltpu.VMEM((2 * STRIP, STRIP), BF16), pltpu.SemaphoreType.DMA((4,))],
        out=HBM,
    )(shares)
    strip, pack = lax.optimization_barrier((strip, pack))
    tables = (2 * STRIP, 4 * HALF)
    decode, spot = call(
        decode_kernel,
        [SMEM, VMEM],
        [(AHEAD, *tables), (8, STRIP)],
        [BF16, jnp.int32],
        turned_scratch,
        moved=3 << 20,
        out=[VMEM] * 2,
    )(column_place, pack)
    strips = lax.all_to_all(strip, line, 0, 0, axis_index_groups=gather)
    partial = call(
        subgrid_kernel,
        [VMEM] * 3,
        (8, STRIP, STRIP),
        BF16,
        [pltpu.VMEM((8 - AHEAD, *tables), BF16), *turned_scratch],
        flops=1 << 29,
    )(strips, decode, pack)
    received = lax.all_to_all(partial, line, 0, 0, axis_index_groups=reduce)
    subgrid = call(
        place_kernel,
        [VMEM, VMEM],
        (2, SUBGRID, STRIP),
        F32,
        [pltpu.VMEM((2, SUBGRID + STRIP, STRIP), F32), pltpu.SemaphoreType.DMA((2,))],
        out=HBM,
    )(spot, received)
    return subgrid.reshape(1, 1, 2, SUBGRID, STRIP)


def solution(mesh):
    split = Mesh(mesh.devices.reshape(SIZES), SPLIT)
    in_specs = (P(None, COL, FAC), P(COL), P(), P(), P(), P(), P())
    return jax.shard_map(
        on_device,
        mesh=split,
        in_specs=in_specs,
        out_specs=P(COL, FAC, None, None, None),
        check_vma=False,
    )
```

time: 72.8 us -> 70.9 us (0.974)
  the two profiles are of different devices: /device:TPU:64 before, /device:TPU:2 now
where the time goes in v4:
time: 70.9 us; the launch traced here: 70.5 us
  blocking collectives  49.2 us (69%)
  Pallas kernels  8.09 us (11%)
  starting transfers between devices  6.38 us (9%)
  waiting for transfers between devices  5.16 us (7%)
  local copies, waits for them, and re-layouts  0.97 us (1%)
  between operations  0.73 us (1%)
    all_to_all x1, blocking collectives, on_device(): received = lax.all_to_all(partial, line, 0, 0, axis_index_groups=reduce)  29.7 us
    all_to_all x1, blocking collectives, on_device(): shares = lax.all_to_all(shares, ('xh', 'y', 'xl'), 0, 0)  19.5 us
    all_to_all x1, waiting for transfers between devices, on_device(): strips = lax.all_to_all(strip, line, 0, 0, axis_index_groups=gather)  5.15 us
    all_to_all x1, starting transfers between devices, on_device(): strips = lax.all_to_all(strip, line, 0, 0, axis_index_groups=gather)  4.46 us
    pallas_call x1, Pallas kernels, prepare(): pl.pallas_call(prepare_kernel, out_shape=(jax.ShapeDtypeStruct((2 * STRIP...  1.92 us
    ppermute x1, starting transfers between devices, on_device(): other = lax.ppermute(own, 'core', [(0, 1), (1, 0)])  1.92 us
    pallas_call x1, Pallas kernels, on_device(): call(subgrid_kernel, [VMEM] * 3, (8, STRIP, STRIP), BF16, [pltpu.VMEM((8...  1.71 us
  transfers between devices with their start and end apart: 2, of which 1 were waited for; matrix products, arithmetic and copies ran while one was open for 0% of the time, Pallas kernels for 3%

profile of v4, /device:TPU:2, one launch (start us, length us, event | category | flops | bytes accessed | tf_op | source)
XLA Modules:
  0.0 70.5 jit_solution(10024395137464932081)
XLA Ops:
  0.0 1.9 %shard_map.82 = (bf16[256,256]{1,0:T(8,128)(2,1)}, f32[320,256]{1,0:T(8,128)}, f32[64,256]{1,0:T(8,128)}) custom-call(bf16[2,256,128]{2,1,0:T(8,128)(2,1)} %facets_hbm.1, f32[1,256]{1,0:T(1,128)} %bitcast.4, f32[32,128]{1,0:T(8,128)} %bitcast.3, s32[16]{0:T(128)} %row_offset_hbm.1, s32[32]{0:T(128)} %offset_hbm.1, s32[16,32]{1,0:T(8,128)} %slot_hbm.1, ...), custom_call_target="tpu_custom_call" | custom-call | bytes 1048576 | tf_op jit(solution)/shard_map/pallas_call | solution.py:276
  1.9 1.9 %collective-permute-start = (bf16[256,256]{1,0:T(8,128)(2,1)}, bf16[256,256]{1,0:T(8,128)(2,1)S(1)}, u32[]{:S(2)}, u32[]{:S(2)}) collective-permute-start(bf16[256,256]{1,0:T(8,128)(2,1)} %get-tuple-element.13), channel_id=1, source_target_pairs={{0,32},{32,0},{1,33},{33,1},{2,34},{34,2},{3,35},{35,3},{4,36},{36... | collective-permute-start | bytes 393224 | tf_op jit(solution)/shard_map/ppermute | solution.py:334
  3.9 0.0 copy-start
  3.9 1.0 %copy-done = f32[320,256]{1,0:T(8,128)S(1)} copy-done((f32[320,256]{1,0:T(8,128)S(1)}, f32[320,256]{1,0:T(8,128)}, u32[]{:S(2)}) %copy-start) | copy-done | bytes 327704
  4.8 0.7 shard_map.83.table_ref
  5.5 0.0 copy-start.1
  5.5 0.0 collective-permute-done.other_ref
  5.5 0.9 %shard_map.84 = bf16[16,128,128]{2,1,0:T(8,128)(2,1)S(1)} custom-call(f32[320,256]{1,0:T(8,128)S(1)} %copy-done, bf16[256,256]{1,0:T(8,128)(2,1)S(1)} %collective-permute-done.other_ref, bf16[8,256,512]{2,1,0:T(8,128)(2,1)S(1)} %shard_map.83.table_ref), custom_call_target="tpu_custom_call" | custom-call | flops 536870912 | bytes 1048576 | tf_op jit(solution)/shard_map/pallas_call | solution.py:338
  6.4 19.5 %all_to_all.15.parts_ref = bf16[16,128,128]{2,1,0:T(8,128)(2,1)S(1)} all-to-all(bf16[16,128,128]{2,1,0:T(8,128)(2,1)S(1)} %shard_map.84), channel_id=1, replica_groups=mesh['xh'=2,'y'=4,'core'=2,'xl'=2,'zh'=4,'zl'=4] {'xh','y','xl'}, dimensions={0} | all-to-all | bytes 1048576 | tf_op jit(solution)/shard_map/all_to_all | solution.py:343
  25.9 0.8 %shard_map.85 = bf16[4,256,128]{2,1,0:T(8,128)(2,1)} custom-call(bf16[16,128,128]{2,1,0:T(8,128)(2,1)S(1)} %all_to_all.15.parts_ref), custom_call_target="tpu_custom_call" | custom-call | bytes 1048576 | tf_op jit(solution)/shard_map/pallas_call | solution.py:344
  26.7 4.5 %all-to-all-start.1 = ((bf16[4,256,128]{2,1,0:T(8,128)(2,1)}), bf16[4,256,128]{2,1,0:T(8,128)(2,1)S(1)}, u32[]{:S(2)}, u32[]{:S(2)}) async-start(bf16[4,256,128]{2,1,0:T(8,128)(2,1)} %shard_map.85), calls=%async_computation.1 | async-start | bytes 524288 | tf_op jit(solution)/shard_map/all_to_all | solution.py:363
  31.9 0.0 copy-done.1
  31.9 1.1 %shard_map.86 = (bf16[6,256,1024]{2,1,0:T(8,128)(2,1)S(1)}, s32[8,128]{1,0:T(8,128)S(1)}) custom-call(s32[1]{0:T(128)S(6)} %copy.9.place_ref, f32[64,256]{1,0:T(8,128)S(1)} %copy-done.1), custom_call_target="tpu_custom_call" | custom-call | bytes 3145728 | tf_op jit(solution)/shard_map/pallas_call | solution.py:354
  33.0 5.2 %all-to-all-done.1.strip_ref = bf16[4,256,128]{2,1,0:T(8,128)(2,1)S(1)} async-done(((bf16[4,256,128]{2,1,0:T(8,128)(2,1)}), bf16[4,256,128]{2,1,0:T(8,128)(2,1)S(1)}, u32[]{:S(2)}, u32[]{:S(2)}) %all-to-all-start.1) | async-done | bytes 262176 | tf_op jit(solution)/shard_map/all_to_all | solution.py:363
  38.1 1.7 %shard_map.87 = bf16[8,128,128]{2,1,0:T(8,128)(2,1)S(1)} custom-call(bf16[4,256,128]{2,1,0:T(8,128)(2,1)S(1)} %all-to-all-done.1.strip_ref, bf16[6,256,1024]{2,1,0:T(8,128)(2,1)S(1)} %get-tuple-element.18.ahead_ref, f32[64,256]{1,0:T(8,128)S(1)} %copy-done.1), custom_call_target="tpu_custom_call" | custom-call | flops 536870912 | bytes 1048576 | tf_op jit(solution)/shard_map/pallas_call | solution.py:364
  39.9 29.7 %all_to_all.16.parts_ref = bf16[8,128,128]{2,1,0:T(8,128)(2,1)S(1)} all-to-all(bf16[8,128,128]{2,1,0:T(8,128)(2,1)S(1)} %shard_map.87), channel_id=1, replica_groups={{15,10,5,0,31,26,21,16},{12,11,6,1,28,27,22,17},{13,8,7,2,29,24,23,18},..., dimensions={0} | all-to-all | bytes 524288 | tf_op jit(solution)/shard_map/all_to_all | solution.py:372
  69.5 1.0 %shard_map.88 = f32[2,512,128]{2,1,0:T(8,128)} custom-call(s32[8,128]{1,0:T(8,128)S(1)} %get-tuple-element.16.place_ref, bf16[8,128,128]{2,1,0:T(8,128)(2,1)S(1)} %all_to_all.16.parts_ref), custom_call_target="tpu_custom_call" | custom-call | bytes 1048576 | tf_op jit(solution)/shard_map/pallas_call | solution.py:373
Async XLA Ops:
  1.9 3.6 %collective-permute-start = (bf16[256,256]{1,0:T(8,128)(2,1)}, bf16[256,256]{1,0:T(8,128)(2,1)S(1)}, u32[]{:S(2)}, u32[]{:S(2)}) collective-permute-start(bf16[256,256]{1,0:T(8,128)(2,1)} %get-tuple-element.13), channel_id=1, source_target_pairs={{0,32},{32,0},{1,33},{33,1},{2,34},{34,2},{3,35},{35,3},{4,36},{36... | collective-permute-start | bytes 393224 | tf_op jit(solution)/shard_map/ppermute | solution.py:334
  3.9 1.0 %copy-start = (f32[320,256]{1,0:T(8,128)S(1)}, f32[320,256]{1,0:T(8,128)}, u32[]{:S(2)}) copy-start(f32[320,256]{1,0:T(8,128)} %get-tuple-element.12.pack_ref.first_ref) | copy-start | bytes 983044
  5.5 26.3 %copy-start.1 = (f32[64,256]{1,0:T(8,128)S(1)}, f32[64,256]{1,0:T(8,128)}, u32[]{:S(2)}) copy-start(f32[64,256]{1,0:T(8,128)} %get-tuple-element.15.pack_ref) | copy-start | bytes 196612
  26.7 11.4 %all-to-all-start.1 = ((bf16[4,256,128]{2,1,0:T(8,128)(2,1)}), bf16[4,256,128]{2,1,0:T(8,128)(2,1)S(1)}, u32[]{:S(2)}, u32[]{:S(2)}) async-start(bf16[4,256,128]{2,1,0:T(8,128)(2,1)} %shard_map.85), calls=%async_computation.1 | async-start | bytes 524288 | tf_op jit(solution)/shard_map/all_to_all | solution.py:363

commit v5 on v4

--- a/solution.py
+++ b/solution.py
@@ -17,8 +17,10 @@
 COL = SPLIT[:3]
 FAC = SPLIT[3:]
 RUN = (0, 1, 2, 3)
-RUNS = ((3, 2, 1, 0), (3, 2, 1, 0))
-TWIST = (0, 1, 2, 3)
+RUNS = ((2, 3, 0, 1), (2, 3, 0, 1))
+TWIST = (0, 2, 2, 0)
+MEMBERS = ((0, 0), (0, 1), (0, 2), (0, 3), (1, 0), (1, 1), (1, 2), (1, 3))
+SHIFT = (2, 0)
 F32 = jnp.float32
 BF16 = jnp.bfloat16
 VMEM = pl.BlockSpec(memory_space=pltpu.VMEM)
@@ -61,8 +63,9 @@
 
 def position():
     core, xl, zh, zl = (lax.axis_index(name) for name in ("core", "xl", "zh", "zl"))
-    place = (4 * zh + zl - 2 * core) & 15
-    return core, xl, place >> 2, place & 3
+    shift = jnp.where(core == 0, *SHIFT)
+    place = (4 * zh + zl - shift) & 15
+    return core, xl, place >> 2, place & 3, shift
 
 
 def spread(starts):
@@ -115,7 +118,7 @@
     sems,
     out_sems,
 ):
-    core, xl, line, step = position()
+    core, xl, line, step, shift = position()
     pair = lax.axis_index("xh") * 4 + lax.axis_index("y")
     fac = (xl * 4 + lax.axis_index("zh")) * 4 + lax.axis_index("zl")
     copies = [
@@ -152,8 +155,8 @@
     for first, second in zip(*RUNS):
         run = jnp.where(core == 0, first, second)
         away = jnp.where(core == 0, TWIST[first], TWIST[second])
-        slots.append((4 * run + 2 * core + ((step - twist + away) & 3)) & 15)
-    slots += [slot + 16 for slot in slots]
+        slots.append((4 * run + shift + ((step - twist + away) & 3)) & 15)
+    slots = [slots[n] + 16 * side for side, n in MEMBERS]
     pack_ref[DECODE] = spread([offset_ref[slot_ref[2 * pair + core, slot] & 31] for slot in slots])
     copies[6].wait()
     first_copy = pltpu.make_async_copy(pack_ref, first_hbm, out_sems.at[1])
@@ -174,8 +177,8 @@
 
 
 def decode_tables(pack_ref, outs, turned_ref):
-    core, _, line, _ = position()
-    blocks = [8 * xl + ((2 * line + core + half) & 7) for xl in range(2) for half in range(2)]
+    _, _, line, _, shift = position()
+    blocks = [8 * xl + ((2 * line + (shift >> 1) + half) & 7) for xl in range(2) for half in range(2)]
     fill_tables(pack_ref, DECODE, STRIP, blocks, outs, turned_ref)
 
 
@@ -236,9 +239,10 @@
     scratch_ref[...] = jnp.zeros_like(scratch_ref)
     halves = []
     for xl in range(2):
-        total = parts_ref[4 * xl].astype(F32)
-        for n in range(1, 4):
-            total += parts_ref[4 * xl + n].astype(F32)
+        first, *others = [n for n in range(8) if MEMBERS[n][0] == xl]
+        total = parts_ref[first].astype(F32)
+        for n in others:
+            total += parts_ref[n].astype(F32)
         halves.append(total)
     low = lax.broadcasted_iota(jnp.int32, (STRIP, STRIP), 1) < STRIP // 2
     copies = []
@@ -301,16 +305,15 @@
 
 def groups():
     gather = [
-        [32 * core + 16 * xl + (4 * n + 2 * core + j) % 16 for j in RUN]
+        [32 * core + 16 * xl + (4 * n + SHIFT[core] + j) % 16 for j in RUN]
         for core in range(2)
         for xl in range(2)
         for n in range(4)
     ]
     reduce = [
         [
-            32 * core + 16 * xl + (4 * n + 2 * core + (s + TWIST[n]) % 4) % 16
-            for xl in range(2)
-            for n in RUNS[core]
+            32 * core + 16 * xl + (4 * n + SHIFT[core] + (s + TWIST[n]) % 4) % 16
+            for xl, n in ((xl, RUNS[core][n]) for xl, n in MEMBERS)
         ]
         for core in range(2)
         for s in range(4)

time: 70.9 us -> 67.9 us (0.958)
  blocking collectives: 49.2 us -> 40.2 us
  starting transfers between devices: 6.38 us -> 13.8 us
  waiting for transfers between devices: 5.16 us -> 3.76 us
    all_to_all x1, blocking collectives: 29.7 us -> 20.6 us  [on_device(): received = lax.all_to_all(partial, line, 0, 0, axis_index_groups=reduce)]
    all_to_all x1, starting transfers between devices: 4.46 us -> 11.9 us  [on_device(): strips = lax.all_to_all(strip, line, 0, 0, axis_index_groups=gather)]
    all_to_all x1, waiting for transfers between devices: 5.15 us -> 3.76 us  [on_device(): strips = lax.all_to_all(strip, line, 0, 0, axis_index_groups=gather)]
where the time goes in v5:
time: 67.9 us; the launch traced here: 67.5 us
  blocking collectives  40.2 us (59%)
  starting transfers between devices  13.8 us (20%)
  Pallas kernels  8.07 us (12%)
  waiting for transfers between devices  3.76 us (6%)
  local copies, waits for them, and re-layouts  0.97 us (1%)
  between operations  0.73 us (1%)
    all_to_all x1, blocking collectives, on_device(): received = lax.all_to_all(partial, line, 0, 0, axis_index_groups=reduce)  20.6 us
    all_to_all x1, blocking collectives, on_device(): shares = lax.all_to_all(shares, ('xh', 'y', 'xl'), 0, 0)  19.5 us
    all_to_all x1, starting transfers between devices, on_device(): strips = lax.all_to_all(strip, line, 0, 0, axis_index_groups=gather)  11.9 us
    all_to_all x1, waiting for transfers between devices, on_device(): strips = lax.all_to_all(strip, line, 0, 0, axis_index_groups=gather)  3.76 us
    pallas_call x1, Pallas kernels, prepare(): pl.pallas_call(prepare_kernel, out_shape=(jax.ShapeDtypeStruct((2 * STRIP...  1.92 us
    ppermute x1, starting transfers between devices, on_device(): other = lax.ppermute(own, 'core', [(0, 1), (1, 0)])  1.92 us
    pallas_call x1, Pallas kernels, on_device(): call(subgrid_kernel, [VMEM] * 3, (8, STRIP, STRIP), BF16, [pltpu.VMEM((8...  1.7 us
  transfers between devices with their start and end apart: 2, of which 1 were waited for; matrix products, arithmetic and copies ran while one was open for 0% of the time, Pallas kernels for 3%

profile of v5, /device:TPU:2, one launch (start us, length us, event | category | flops | bytes accessed | tf_op | source)
XLA Modules:
  0.0 67.5 jit_solution(146865700610174780)
XLA Ops:
  0.0 1.9 %shard_map.82 = (bf16[256,256]{1,0:T(8,128)(2,1)}, f32[320,256]{1,0:T(8,128)}, f32[64,256]{1,0:T(8,128)}) custom-call(bf16[2,256,128]{2,1,0:T(8,128)(2,1)} %facets_hbm.1, f32[1,256]{1,0:T(1,128)} %bitcast.4, f32[32,128]{1,0:T(8,128)} %bitcast.3, s32[16]{0:T(128)} %row_offset_hbm.1, s32[32]{0:T(128)} %offset_hbm.1, s32[16,32]{1,0:T(8,128)} %slot_hbm.1, ...), custom_call_target="tpu_custom_call" | custom-call | bytes 1048576 | tf_op jit(solution)/shard_map/pallas_call | solution.py:280
  1.9 1.9 %collective-permute-start = (bf16[256,256]{1,0:T(8,128)(2,1)}, bf16[256,256]{1,0:T(8,128)(2,1)S(1)}, u32[]{:S(2)}, u32[]{:S(2)}) collective-permute-start(bf16[256,256]{1,0:T(8,128)(2,1)} %get-tuple-element.13), channel_id=1, source_target_pairs={{0,32},{32,0},{1,33},{33,1},{2,34},{34,2},{3,35},{35,3},{4,36},{36... | collective-permute-start | bytes 393224 | tf_op jit(solution)/shard_map/ppermute | solution.py:337
  3.9 0.0 copy-start
  3.9 1.0 %copy-done = f32[320,256]{1,0:T(8,128)S(1)} copy-done((f32[320,256]{1,0:T(8,128)S(1)}, f32[320,256]{1,0:T(8,128)}, u32[]{:S(2)}) %copy-start) | copy-done | bytes 327704
  4.8 0.7 shard_map.83.table_ref
  5.5 0.0 copy-start.1
  5.5 0.0 collective-permute-done.other_ref
  5.5 0.8 %shard_map.84 = bf16[16,128,128]{2,1,0:T(8,128)(2,1)S(1)} custom-call(f32[320,256]{1,0:T(8,128)S(1)} %copy-done, bf16[256,256]{1,0:T(8,128)(2,1)S(1)} %collective-permute-done.other_ref, bf16[8,256,512]{2,1,0:T(8,128)(2,1)S(1)} %shard_map.83.table_ref), custom_call_target="tpu_custom_call" | custom-call | flops 536870912 | bytes 1048576 | tf_op jit(solution)/shard_map/pallas_call | solution.py:341
  6.4 19.5 %all_to_all.15.parts_ref = bf16[16,128,128]{2,1,0:T(8,128)(2,1)S(1)} all-to-all(bf16[16,128,128]{2,1,0:T(8,128)(2,1)S(1)} %shard_map.84), channel_id=1, replica_groups=mesh['xh'=2,'y'=4,'core'=2,'xl'=2,'zh'=4,'zl'=4] {'xh','y','xl'}, dimensions={0} | all-to-all | bytes 1048576 | tf_op jit(solution)/shard_map/all_to_all | solution.py:346
  25.9 0.8 %shard_map.85 = bf16[4,256,128]{2,1,0:T(8,128)(2,1)} custom-call(bf16[16,128,128]{2,1,0:T(8,128)(2,1)S(1)} %all_to_all.15.parts_ref), custom_call_target="tpu_custom_call" | custom-call | bytes 1048576 | tf_op jit(solution)/shard_map/pallas_call | solution.py:347
  26.7 11.9 %all-to-all-start.1 = ((bf16[4,256,128]{2,1,0:T(8,128)(2,1)}), bf16[4,256,128]{2,1,0:T(8,128)(2,1)S(1)}, u32[]{:S(2)}, u32[]{:S(2)}) async-start(bf16[4,256,128]{2,1,0:T(8,128)(2,1)} %shard_map.85), calls=%async_computation.1 | async-start | bytes 524288 | tf_op jit(solution)/shard_map/all_to_all | solution.py:366
  39.3 0.0 copy-done.1
  39.3 1.1 %shard_map.86 = (bf16[6,256,1024]{2,1,0:T(8,128)(2,1)S(1)}, s32[8,128]{1,0:T(8,128)S(1)}) custom-call(s32[1]{0:T(128)S(6)} %copy.9.place_ref, f32[64,256]{1,0:T(8,128)S(1)} %copy-done.1), custom_call_target="tpu_custom_call" | custom-call | bytes 3145728 | tf_op jit(solution)/shard_map/pallas_call | solution.py:357
  40.4 3.8 %all-to-all-done.1.strip_ref = bf16[4,256,128]{2,1,0:T(8,128)(2,1)S(1)} async-done(((bf16[4,256,128]{2,1,0:T(8,128)(2,1)}), bf16[4,256,128]{2,1,0:T(8,128)(2,1)S(1)}, u32[]{:S(2)}, u32[]{:S(2)}) %all-to-all-start.1) | async-done | bytes 262176 | tf_op jit(solution)/shard_map/all_to_all | solution.py:366
  44.2 1.7 %shard_map.87 = bf16[8,128,128]{2,1,0:T(8,128)(2,1)S(1)} custom-call(bf16[4,256,128]{2,1,0:T(8,128)(2,1)S(1)} %all-to-all-done.1.strip_ref, bf16[6,256,1024]{2,1,0:T(8,128)(2,1)S(1)} %get-tuple-element.18.ahead_ref, f32[64,256]{1,0:T(8,128)S(1)} %copy-done.1), custom_call_target="tpu_custom_call" | custom-call | flops 536870912 | bytes 1048576 | tf_op jit(solution)/shard_map/pallas_call | solution.py:367
  45.9 20.6 %all_to_all.16.parts_ref = bf16[8,128,128]{2,1,0:T(8,128)(2,1)S(1)} all-to-all(bf16[8,128,128]{2,1,0:T(8,128)(2,1)S(1)} %shard_map.87), channel_id=1, replica_groups={{12,14,2,8,28,30,18,24},{13,15,3,9,29,31,19,25},{10,0,4,6,26,16,20,22},..., dimensions={0} | all-to-all | bytes 524288 | tf_op jit(solution)/shard_map/all_to_all | solution.py:375
  66.5 1.0 %shard_map.88 = f32[2,512,128]{2,1,0:T(8,128)} custom-call(s32[8,128]{1,0:T(8,128)S(1)} %get-tuple-element.16.place_ref, bf16[8,128,128]{2,1,0:T(8,128)(2,1)S(1)} %all_to_all.16.parts_ref), custom_call_target="tpu_custom_call" | custom-call | bytes 1048576 | tf_op jit(solution)/shard_map/pallas_call | solution.py:376
Async XLA Ops:
  1.9 3.6 %collective-permute-start = (bf16[256,256]{1,0:T(8,128)(2,1)}, bf16[256,256]{1,0:T(8,128)(2,1)S(1)}, u32[]{:S(2)}, u32[]{:S(2)}) collective-permute-start(bf16[256,256]{1,0:T(8,128)(2,1)} %get-tuple-element.13), channel_id=1, source_target_pairs={{0,32},{32,0},{1,33},{33,1},{2,34},{34,2},{3,35},{35,3},{4,36},{36... | collective-permute-start | bytes 393224 | tf_op jit(solution)/shard_map/ppermute | solution.py:337
  3.9 1.0 %copy-start = (f32[320,256]{1,0:T(8,128)S(1)}, f32[320,256]{1,0:T(8,128)}, u32[]{:S(2)}) copy-start(f32[320,256]{1,0:T(8,128)} %get-tuple-element.12.pack_ref.first_ref) | copy-start | bytes 983044
  5.5 33.8 %copy-start.1 = (f32[64,256]{1,0:T(8,128)S(1)}, f32[64,256]{1,0:T(8,128)}, u32[]{:S(2)}) copy-start(f32[64,256]{1,0:T(8,128)} %get-tuple-element.15.pack_ref) | copy-start | bytes 196612
  26.7 17.4 %all-to-all-start.1 = ((bf16[4,256,128]{2,1,0:T(8,128)(2,1)}), bf16[4,256,128]{2,1,0:T(8,128)(2,1)S(1)}, u32[]{:S(2)}, u32[]{:S(2)}) async-start(bf16[4,256,128]{2,1,0:T(8,128)(2,1)} %shard_map.85), calls=%async_computation.1 | async-start | bytes 524288 | tf_op jit(solution)/shard_map/all_to_all | solution.py:366

commit v6 on v5

--- a/solution.py
+++ b/solution.py
@@ -16,8 +16,9 @@
 SIZES = (2, 4, 2, 2, 4, 4)
 COL = SPLIT[:3]
 FAC = SPLIT[3:]
+PLANE = tuple(range(15, -1, -1))
 RUN = (0, 1, 2, 3)
-RUNS = ((2, 3, 0, 1), (2, 3, 0, 1))
+RUNS = ((2, 3, 1, 0), (2, 3, 1, 0))
 TWIST = (0, 2, 2, 0)
 MEMBERS = ((0, 0), (0, 1), (0, 2), (0, 3), (1, 0), (1, 1), (1, 2), (1, 3))
 SHIFT = (2, 0)
@@ -203,14 +204,15 @@
         )
         for half in range(2):
             part = product[:, STRIP * half : STRIP * (half + 1)]
-            out_ref[2 * n + half] = joined(part[:STRIP], part[STRIP:]).astype(BF16)
+            out_ref[PLANE.index(2 * n + half)] = joined(part[:STRIP], part[STRIP:]).astype(BF16)
 
 
 def sum_kernel(parts_ref, out_hbm, total_ref, sems):
     for xl in range(2):
-        total = parts_ref[xl].astype(F32)
-        for n in range(1, 8):
-            total += parts_ref[2 * n + xl].astype(F32)
+        first, *others = [PLANE.index(2 * n + xl) for n in range(8)]
+        total = parts_ref[first].astype(F32)
+        for n in others:
+            total += parts_ref[n].astype(F32)
         total_ref[STRIP * xl : STRIP * (xl + 1), :] = total.astype(BF16)
     copies = [pltpu.make_async_copy(total_ref, out_hbm.at[n], sems.at[n]) for n in range(4)]
     for copy in copies:
@@ -343,7 +345,7 @@
     )
     gather, reduce = groups()
     line = ("core",) + FAC
-    shares = lax.all_to_all(shares, ("xh", "y", "xl"), 0, 0)
+    shares = lax.all_to_all(shares, ("xh", "y", "xl"), 0, 0, axis_index_groups=[list(PLANE)])
     strip = call(
         sum_kernel,
         [VMEM],

time: 67.9 us -> 66.2 us (0.975)
  the two profiles are of different devices: /device:TPU:2 before, /device:TPU:4 now
where the time goes in v6:
time: 66.2 us; the launch traced here: 65.8 us
  blocking collectives  40.1 us (61%)
  starting transfers between devices  11.8 us (18%)
  Pallas kernels  8.08 us (12%)
  waiting for transfers between devices  4.12 us (6%)
  local copies, waits for them, and re-layouts  0.97 us (1%)
  between operations  0.73 us (1%)
    all_to_all x1, blocking collectives, on_device(): received = lax.all_to_all(partial, line, 0, 0, axis_index_groups=reduce)  20.4 us
    all_to_all x1, blocking collectives, on_device(): lax.all_to_all(shares, ('xh', 'y', 'xl'), 0, 0, axis_index_groups=[list(P...  19.7 us
    all_to_all x1, starting transfers between devices, on_device(): strips = lax.all_to_all(strip, line, 0, 0, axis_index_groups=gather)  9.91 us
    all_to_all x1, waiting for transfers between devices, on_device(): strips = lax.all_to_all(strip, line, 0, 0, axis_index_groups=gather)  4.12 us
    pallas_call x1, Pallas kernels, prepare(): pl.pallas_call(prepare_kernel, out_shape=(jax.ShapeDtypeStruct((2 * STRIP...  1.92 us
    ppermute x1, starting transfers between devices, on_device(): other = lax.ppermute(own, 'core', [(0, 1), (1, 0)])  1.92 us
    pallas_call x1, Pallas kernels, on_device(): call(subgrid_kernel, [VMEM] * 3, (8, STRIP, STRIP), BF16, [pltpu.VMEM((8...  1.7 us
  transfers between devices with their start and end apart: 2, of which 1 were waited for; matrix products, arithmetic and copies ran while one was open for 0% of the time, Pallas kernels for 3%

profile of v6, /device:TPU:4, one launch (start us, length us, event | category | flops | bytes accessed | tf_op | source)
XLA Modules:
  0.0 65.8 jit_solution(3672788936690142483)
XLA Ops:
  0.0 1.9 %shard_map.82 = (bf16[256,256]{1,0:T(8,128)(2,1)}, f32[320,256]{1,0:T(8,128)}, f32[64,256]{1,0:T(8,128)}) custom-call(bf16[2,256,128]{2,1,0:T(8,128)(2,1)} %facets_hbm.1, f32[1,256]{1,0:T(1,128)} %bitcast.4, f32[32,128]{1,0:T(8,128)} %bitcast.3, s32[16]{0:T(128)} %row_offset_hbm.1, s32[32]{0:T(128)} %offset_hbm.1, s32[16,32]{1,0:T(8,128)} %slot_hbm.1, ...), custom_call_target="tpu_custom_call" | custom-call | bytes 1048576 | tf_op jit(solution)/shard_map/pallas_call | solution.py:282
  1.9 1.9 %collective-permute-start = (bf16[256,256]{1,0:T(8,128)(2,1)}, bf16[256,256]{1,0:T(8,128)(2,1)S(1)}, u32[]{:S(2)}, u32[]{:S(2)}) collective-permute-start(bf16[256,256]{1,0:T(8,128)(2,1)} %get-tuple-element.13), channel_id=1, source_target_pairs={{0,32},{32,0},{1,33},{33,1},{2,34},{34,2},{3,35},{35,3},{4,36},{36... | collective-permute-start | bytes 393224 | tf_op jit(solution)/shard_map/ppermute | solution.py:339
  3.9 0.0 copy-start
  3.9 1.0 %copy-done = f32[320,256]{1,0:T(8,128)S(1)} copy-done((f32[320,256]{1,0:T(8,128)S(1)}, f32[320,256]{1,0:T(8,128)}, u32[]{:S(2)}) %copy-start) | copy-done | bytes 327704
  4.8 0.7 %shard_map.83.table_ref = bf16[8,256,512]{2,1,0:T(8,128)(2,1)S(1)} custom-call(f32[320,256]{1,0:T(8,128)S(1)} %copy-done), custom_call_target="tpu_custom_call" | custom-call | bytes 3145728 | tf_op jit(solution)/shard_map/pallas_call | solution.py:340
  5.5 0.0 copy-start.1
  5.5 0.0 collective-permute-done.other_ref
  5.5 0.9 %shard_map.84 = bf16[16,128,128]{2,1,0:T(8,128)(2,1)S(1)} custom-call(f32[320,256]{1,0:T(8,128)S(1)} %copy-done, bf16[256,256]{1,0:T(8,128)(2,1)S(1)} %collective-permute-done.other_ref, bf16[8,256,512]{2,1,0:T(8,128)(2,1)S(1)} %shard_map.83.table_ref), custom_call_target="tpu_custom_call" | custom-call | flops 536870912 | bytes 1048576 | tf_op jit(solution)/shard_map/pallas_call | solution.py:343
  6.4 19.7 %all_to_all.15.parts_ref = bf16[16,128,128]{2,1,0:T(8,128)(2,1)S(1)} all-to-all(bf16[16,128,128]{2,1,0:T(8,128)(2,1)S(1)} %shard_map.84), channel_id=1, replica_groups={{464,448,400,384,336,320,272,256,208,192,144,128,80,64,16,0},{465,449,4..., dimensions={0} | all-to-all | bytes 1048576 | tf_op jit(solution)/shard_map/all_to_all | solution.py:348
  26.1 0.8 %shard_map.85 = bf16[4,256,128]{2,1,0:T(8,128)(2,1)} custom-call(bf16[16,128,128]{2,1,0:T(8,128)(2,1)S(1)} %all_to_all.15.parts_ref), custom_call_target="tpu_custom_call" | custom-call | bytes 1048576 | tf_op jit(solution)/shard_map/pallas_call | solution.py:349
  26.9 9.9 %all-to-all-start.1 = ((bf16[4,256,128]{2,1,0:T(8,128)(2,1)}), bf16[4,256,128]{2,1,0:T(8,128)(2,1)S(1)}, u32[]{:S(2)}, u32[]{:S(2)}) async-start(bf16[4,256,128]{2,1,0:T(8,128)(2,1)} %shard_map.85), calls=%async_computation.1 | async-start | bytes 524288 | tf_op jit(solution)/shard_map/all_to_all | solution.py:368
  37.5 0.0 copy-done.1
  37.5 1.1 %shard_map.86 = (bf16[6,256,1024]{2,1,0:T(8,128)(2,1)S(1)}, s32[8,128]{1,0:T(8,128)S(1)}) custom-call(s32[1]{0:T(128)S(6)} %copy.9.place_ref, f32[64,256]{1,0:T(8,128)S(1)} %copy-done.1), custom_call_target="tpu_custom_call" | custom-call | bytes 3145728 | tf_op jit(solution)/shard_map/pallas_call | solution.py:359
  38.6 4.1 %all-to-all-done.1.strip_ref = bf16[4,256,128]{2,1,0:T(8,128)(2,1)S(1)} async-done(((bf16[4,256,128]{2,1,0:T(8,128)(2,1)}), bf16[4,256,128]{2,1,0:T(8,128)(2,1)S(1)}, u32[]{:S(2)}, u32[]{:S(2)}) %all-to-all-start.1) | async-done | bytes 262176 | tf_op jit(solution)/shard_map/all_to_all | solution.py:368
  42.7 1.7 %shard_map.87 = bf16[8,128,128]{2,1,0:T(8,128)(2,1)S(1)} custom-call(bf16[4,256,128]{2,1,0:T(8,128)(2,1)S(1)} %all-to-all-done.1.strip_ref, bf16[6,256,1024]{2,1,0:T(8,128)(2,1)S(1)} %get-tuple-element.18.ahead_ref, f32[64,256]{1,0:T(8,128)S(1)} %copy-done.1), custom_call_target="tpu_custom_call" | custom-call | flops 536870912 | bytes 1048576 | tf_op jit(solution)/shard_map/pallas_call | solution.py:369
  44.4 20.4 %all_to_all.16.parts_ref = bf16[8,128,128]{2,1,0:T(8,128)(2,1)S(1)} all-to-all(bf16[8,128,128]{2,1,0:T(8,128)(2,1)S(1)} %shard_map.87), channel_id=1, replica_groups={{12,14,8,2,28,30,24,18},{13,15,9,3,29,31,25,19},{10,0,6,4,26,16,22,20},..., dimensions={0} | all-to-all | bytes 524288 | tf_op jit(solution)/shard_map/all_to_all | solution.py:377
  64.8 1.0 %shard_map.88 = f32[2,512,128]{2,1,0:T(8,128)} custom-call(s32[8,128]{1,0:T(8,128)S(1)} %get-tuple-element.16.place_ref, bf16[8,128,128]{2,1,0:T(8,128)(2,1)S(1)} %all_to_all.16.parts_ref), custom_call_target="tpu_custom_call" | custom-call | bytes 1048576 | tf_op jit(solution)/shard_map/pallas_call | solution.py:378
Async XLA Ops:
  1.9 3.6 %collective-permute-start = (bf16[256,256]{1,0:T(8,128)(2,1)}, bf16[256,256]{1,0:T(8,128)(2,1)S(1)}, u32[]{:S(2)}, u32[]{:S(2)}) collective-permute-start(bf16[256,256]{1,0:T(8,128)(2,1)} %get-tuple-element.13), channel_id=1, source_target_pairs={{0,32},{32,0},{1,33},{33,1},{2,34},{34,2},{3,35},{35,3},{4,36},{36... | collective-permute-start | bytes 393224 | tf_op jit(solution)/shard_map/ppermute | solution.py:339
  3.9 1.0 %copy-start = (f32[320,256]{1,0:T(8,128)S(1)}, f32[320,256]{1,0:T(8,128)}, u32[]{:S(2)}) copy-start(f32[320,256]{1,0:T(8,128)} %get-tuple-element.12.pack_ref.first_ref) | copy-start | bytes 983044
  5.5 32.0 %copy-start.1 = (f32[64,256]{1,0:T(8,128)S(1)}, f32[64,256]{1,0:T(8,128)}, u32[]{:S(2)}) copy-start(f32[64,256]{1,0:T(8,128)} %get-tuple-element.15.pack_ref) | copy-start | bytes 196612
  26.9 15.8 %all-to-all-start.1 = ((bf16[4,256,128]{2,1,0:T(8,128)(2,1)}), bf16[4,256,128]{2,1,0:T(8,128)(2,1)S(1)}, u32[]{:S(2)}, u32[]{:S(2)}) async-start(bf16[4,256,128]{2,1,0:T(8,128)(2,1)} %shard_map.85), calls=%async_computation.1 | async-start | bytes 524288 | tf_op jit(solution)/shard_map/all_to_all | solution.py:368

commit v7 on v6

--- a/solution.py
+++ b/solution.py
@@ -16,7 +16,7 @@
 SIZES = (2, 4, 2, 2, 4, 4)
 COL = SPLIT[:3]
 FAC = SPLIT[3:]
-PLANE = tuple(range(15, -1, -1))
+PLANE = (13, 12, 15, 14, 9, 8, 11, 10, 5, 4, 7, 6, 1, 0, 3, 2)
 RUN = (0, 1, 2, 3)
 RUNS = ((2, 3, 1, 0), (2, 3, 1, 0))
 TWIST = (0, 2, 2, 0)

time: 66.2 us -> 65.7 us (level)
  the two profiles are of different devices: /device:TPU:4 before, /device:TPU:8 now
where the time goes in v7:
time: 65.7 us; the launch traced here: 65.4 us
  blocking collectives  40.1 us (61%)
  starting transfers between devices  11.8 us (18%)
  Pallas kernels  8.08 us (12%)
  waiting for transfers between devices  3.71 us (6%)
  local copies, waits for them, and re-layouts  0.97 us (1%)
  between operations  0.73 us (1%)
    all_to_all x1, blocking collectives, on_device(): received = lax.all_to_all(partial, line, 0, 0, axis_index_groups=reduce)  20.5 us
    all_to_all x1, blocking collectives, on_device(): lax.all_to_all(shares, ('xh', 'y', 'xl'), 0, 0, axis_index_groups=[list(P...  19.6 us
    all_to_all x1, starting transfers between devices, on_device(): strips = lax.all_to_all(strip, line, 0, 0, axis_index_groups=gather)  9.84 us
    all_to_all x1, waiting for transfers between devices, on_device(): strips = lax.all_to_all(strip, line, 0, 0, axis_index_groups=gather)  3.71 us
    pallas_call x1, Pallas kernels, prepare(): pl.pallas_call(prepare_kernel, out_shape=(jax.ShapeDtypeStruct((2 * STRIP...  1.92 us
    ppermute x1, starting transfers between devices, on_device(): other = lax.ppermute(own, 'core', [(0, 1), (1, 0)])  1.92 us
    pallas_call x1, Pallas kernels, on_device(): call(subgrid_kernel, [VMEM] * 3, (8, STRIP, STRIP), BF16, [pltpu.VMEM((8...  1.7 us
  transfers between devices with their start and end apart: 2, of which 1 were waited for; matrix products, arithmetic and copies ran while one was open for 0% of the time, Pallas kernels for 3%

profile of v7, /device:TPU:8, one launch (start us, length us, event | category | flops | bytes accessed | tf_op | source)
XLA Modules:
  0.0 65.4 jit_solution(6206158172516181590)
XLA Ops:
  0.0 1.9 %shard_map.82 = (bf16[256,256]{1,0:T(8,128)(2,1)}, f32[320,256]{1,0:T(8,128)}, f32[64,256]{1,0:T(8,128)}) custom-call(bf16[2,256,128]{2,1,0:T(8,128)(2,1)} %facets_hbm.1, f32[1,256]{1,0:T(1,128)} %bitcast.4, f32[32,128]{1,0:T(8,128)} %bitcast.3, s32[16]{0:T(128)} %row_offset_hbm.1, s32[32]{0:T(128)} %offset_hbm.1, s32[16,32]{1,0:T(8,128)} %slot_hbm.1, ...), custom_call_target="tpu_custom_call" | custom-call | bytes 1048576 | tf_op jit(solution)/shard_map/pallas_call | solution.py:282
  1.9 1.9 %collective-permute-start = (bf16[256,256]{1,0:T(8,128)(2,1)}, bf16[256,256]{1,0:T(8,128)(2,1)S(1)}, u32[]{:S(2)}, u32[]{:S(2)}) collective-permute-start(bf16[256,256]{1,0:T(8,128)(2,1)} %get-tuple-element.13), channel_id=1, source_target_pairs={{0,32},{32,0},{1,33},{33,1},{2,34},{34,2},{3,35},{35,3},{4,36},{36... | collective-permute-start | bytes 393224 | tf_op jit(solution)/shard_map/ppermute | solution.py:339
  3.9 0.0 copy-start
  3.9 1.0 %copy-done = f32[320,256]{1,0:T(8,128)S(1)} copy-done((f32[320,256]{1,0:T(8,128)S(1)}, f32[320,256]{1,0:T(8,128)}, u32[]{:S(2)}) %copy-start) | copy-done | bytes 327704
  4.8 0.7 %shard_map.83.table_ref = bf16[8,256,512]{2,1,0:T(8,128)(2,1)S(1)} custom-call(f32[320,256]{1,0:T(8,128)S(1)} %copy-done), custom_call_target="tpu_custom_call" | custom-call | bytes 3145728 | tf_op jit(solution)/shard_map/pallas_call | solution.py:340
  5.5 0.0 copy-start.1
  5.5 0.0 collective-permute-done.other_ref
  5.5 0.9 %shard_map.84 = bf16[16,128,128]{2,1,0:T(8,128)(2,1)S(1)} custom-call(f32[320,256]{1,0:T(8,128)S(1)} %copy-done, bf16[256,256]{1,0:T(8,128)(2,1)S(1)} %collective-permute-done.other_ref, bf16[8,256,512]{2,1,0:T(8,128)(2,1)S(1)} %shard_map.83.table_ref), custom_call_target="tpu_custom_call" | custom-call | flops 536870912 | bytes 1048576 | tf_op jit(solution)/shard_map/pallas_call | solution.py:343
  6.4 19.6 %all_to_all.15.parts_ref = bf16[16,128,128]{2,1,0:T(8,128)(2,1)S(1)} all-to-all(bf16[16,128,128]{2,1,0:T(8,128)(2,1)S(1)} %shard_map.84), channel_id=1, replica_groups={{400,384,464,448,272,256,336,320,144,128,208,192,16,0,80,64},{401,385,4..., dimensions={0} | all-to-all | bytes 1048576 | tf_op jit(solution)/shard_map/all_to_all | solution.py:348
  26.0 0.8 %shard_map.85 = bf16[4,256,128]{2,1,0:T(8,128)(2,1)} custom-call(bf16[16,128,128]{2,1,0:T(8,128)(2,1)S(1)} %all_to_all.15.parts_ref), custom_call_target="tpu_custom_call" | custom-call | bytes 1048576 | tf_op jit(solution)/shard_map/pallas_call | solution.py:349
  26.8 9.8 %all-to-all-start.1 = ((bf16[4,256,128]{2,1,0:T(8,128)(2,1)}), bf16[4,256,128]{2,1,0:T(8,128)(2,1)S(1)}, u32[]{:S(2)}, u32[]{:S(2)}) async-start(bf16[4,256,128]{2,1,0:T(8,128)(2,1)} %shard_map.85), calls=%async_computation.1 | async-start | bytes 524288 | tf_op jit(solution)/shard_map/all_to_all | solution.py:368
  37.3 0.0 copy-done.1
  37.3 1.1 %shard_map.86 = (bf16[6,256,1024]{2,1,0:T(8,128)(2,1)S(1)}, s32[8,128]{1,0:T(8,128)S(1)}) custom-call(s32[1]{0:T(128)S(6)} %copy.9.place_ref, f32[64,256]{1,0:T(8,128)S(1)} %copy-done.1), custom_call_target="tpu_custom_call" | custom-call | bytes 3145728 | tf_op jit(solution)/shard_map/pallas_call | solution.py:359
  38.4 3.7 %all-to-all-done.1.strip_ref = bf16[4,256,128]{2,1,0:T(8,128)(2,1)S(1)} async-done(((bf16[4,256,128]{2,1,0:T(8,128)(2,1)}), bf16[4,256,128]{2,1,0:T(8,128)(2,1)S(1)}, u32[]{:S(2)}, u32[]{:S(2)}) %all-to-all-start.1) | async-done | bytes 262176 | tf_op jit(solution)/shard_map/all_to_all | solution.py:368
  42.1 1.7 %shard_map.87 = bf16[8,128,128]{2,1,0:T(8,128)(2,1)S(1)} custom-call(bf16[4,256,128]{2,1,0:T(8,128)(2,1)S(1)} %all-to-all-done.1.strip_ref, bf16[6,256,1024]{2,1,0:T(8,128)(2,1)S(1)} %get-tuple-element.18.ahead_ref, f32[64,256]{1,0:T(8,128)S(1)} %copy-done.1), custom_call_target="tpu_custom_call" | custom-call | flops 536870912 | bytes 1048576 | tf_op jit(solution)/shard_map/pallas_call | solution.py:369
  43.8 20.5 %all_to_all.16.parts_ref = bf16[8,128,128]{2,1,0:T(8,128)(2,1)S(1)} all-to-all(bf16[8,128,128]{2,1,0:T(8,128)(2,1)S(1)} %shard_map.87), channel_id=1, replica_groups={{12,14,8,2,28,30,24,18},{13,15,9,3,29,31,25,19},{10,0,6,4,26,16,22,20},..., dimensions={0} | all-to-all | bytes 524288 | tf_op jit(solution)/shard_map/all_to_all | solution.py:377
  64.3 1.0 %shard_map.88 = f32[2,512,128]{2,1,0:T(8,128)} custom-call(s32[8,128]{1,0:T(8,128)S(1)} %get-tuple-element.16.place_ref, bf16[8,128,128]{2,1,0:T(8,128)(2,1)S(1)} %all_to_all.16.parts_ref), custom_call_target="tpu_custom_call" | custom-call | bytes 1048576 | tf_op jit(solution)/shard_map/pallas_call | solution.py:378
Async XLA Ops:
  1.9 3.6 %collective-permute-start = (bf16[256,256]{1,0:T(8,128)(2,1)}, bf16[256,256]{1,0:T(8,128)(2,1)S(1)}, u32[]{:S(2)}, u32[]{:S(2)}) collective-permute-start(bf16[256,256]{1,0:T(8,128)(2,1)} %get-tuple-element.13), channel_id=1, source_target_pairs={{0,32},{32,0},{1,33},{33,1},{2,34},{34,2},{3,35},{35,3},{4,36},{36... | collective-permute-start | bytes 393224 | tf_op jit(solution)/shard_map/ppermute | solution.py:339
  3.9 1.0 %copy-start = (f32[320,256]{1,0:T(8,128)S(1)}, f32[320,256]{1,0:T(8,128)}, u32[]{:S(2)}) copy-start(f32[320,256]{1,0:T(8,128)} %get-tuple-element.12.pack_ref.first_ref) | copy-start | bytes 983044
  5.5 31.8 %copy-start.1 = (f32[64,256]{1,0:T(8,128)S(1)}, f32[64,256]{1,0:T(8,128)}, u32[]{:S(2)}) copy-start(f32[64,256]{1,0:T(8,128)} %get-tuple-element.15.pack_ref) | copy-start | bytes 196612
  26.8 15.3 %all-to-all-start.1 = ((bf16[4,256,128]{2,1,0:T(8,128)(2,1)}), bf16[4,256,128]{2,1,0:T(8,128)(2,1)S(1)}, u32[]{:S(2)}, u32[]{:S(2)}) async-start(bf16[4,256,128]{2,1,0:T(8,128)(2,1)} %shard_map.85), calls=%async_computation.1 | async-start | bytes 524288 | tf_op jit(solution)/shard_map/all_to_all | solution.py:368

commit v8 on v7

--- a/solution.py
+++ b/solution.py
@@ -19,7 +19,7 @@
 PLANE = (13, 12, 15, 14, 9, 8, 11, 10, 5, 4, 7, 6, 1, 0, 3, 2)
 RUN = (0, 1, 2, 3)
 RUNS = ((2, 3, 1, 0), (2, 3, 1, 0))
-TWIST = (0, 2, 2, 0)
+TWIST = (0, 0, 2, 2)
 MEMBERS = ((0, 0), (0, 1), (0, 2), (0, 3), (1, 0), (1, 1), (1, 2), (1, 3))
 SHIFT = (2, 0)
 F32 = jnp.float32

time: 65.7 us -> 65.2 us (level)
  no operation moved by 1% of the time
where the time goes in v8:
time: 65.2 us; the launch traced here: 64.8 us
  blocking collectives  39.6 us (61%)
  starting transfers between devices  11.8 us (18%)
  Pallas kernels  8.08 us (12%)
  waiting for transfers between devices  3.71 us (6%)
  local copies, waits for them, and re-layouts  0.97 us (1%)
  between operations  0.73 us (1%)
    all_to_all x1, blocking collectives, on_device(): received = lax.all_to_all(partial, line, 0, 0, axis_index_groups=reduce)  20 us
    all_to_all x1, blocking collectives, on_device(): lax.all_to_all(shares, ('xh', 'y', 'xl'), 0, 0, axis_index_groups=[list(P...  19.6 us
    all_to_all x1, starting transfers between devices, on_device(): strips = lax.all_to_all(strip, line, 0, 0, axis_index_groups=gather)  9.84 us
    all_to_all x1, waiting for transfers between devices, on_device(): strips = lax.all_to_all(strip, line, 0, 0, axis_index_groups=gather)  3.71 us
    pallas_call x1, Pallas kernels, prepare(): pl.pallas_call(prepare_kernel, out_shape=(jax.ShapeDtypeStruct((2 * STRIP...  1.92 us
    ppermute x1, starting transfers between devices, on_device(): other = lax.ppermute(own, 'core', [(0, 1), (1, 0)])  1.92 us
    pallas_call x1, Pallas kernels, on_device(): call(subgrid_kernel, [VMEM] * 3, (8, STRIP, STRIP), BF16, [pltpu.VMEM((8...  1.7 us
  transfers between devices with their start and end apart: 2, of which 1 were waited for; matrix products, arithmetic and copies ran while one was open for 0% of the time, Pallas kernels for 3%

profile of v8, /device:TPU:8, one launch (start us, length us, event | category | flops | bytes accessed | tf_op | source)
XLA Modules:
  0.0 64.8 jit_solution(16390100305418411637)
XLA Ops:
  0.0 1.9 %shard_map.82 = (bf16[256,256]{1,0:T(8,128)(2,1)}, f32[320,256]{1,0:T(8,128)}, f32[64,256]{1,0:T(8,128)}) custom-call(bf16[2,256,128]{2,1,0:T(8,128)(2,1)} %facets_hbm.1, f32[1,256]{1,0:T(1,128)} %bitcast.4, f32[32,128]{1,0:T(8,128)} %bitcast.3, s32[16]{0:T(128)} %row_offset_hbm.1, s32[32]{0:T(128)} %offset_hbm.1, s32[16,32]{1,0:T(8,128)} %slot_hbm.1, ...), custom_call_target="tpu_custom_call" | custom-call | bytes 1048576 | tf_op jit(solution)/shard_map/pallas_call | solution.py:282
  1.9 1.9 %collective-permute-start = (bf16[256,256]{1,0:T(8,128)(2,1)}, bf16[256,256]{1,0:T(8,128)(2,1)S(1)}, u32[]{:S(2)}, u32[]{:S(2)}) collective-permute-start(bf16[256,256]{1,0:T(8,128)(2,1)} %get-tuple-element.13), channel_id=1, source_target_pairs={{0,32},{32,0},{1,33},{33,1},{2,34},{34,2},{3,35},{35,3},{4,36},{36... | collective-permute-start | bytes 393224 | tf_op jit(solution)/shard_map/ppermute | solution.py:339
  3.9 0.0 copy-start
  3.9 1.0 %copy-done = f32[320,256]{1,0:T(8,128)S(1)} copy-done((f32[320,256]{1,0:T(8,128)S(1)}, f32[320,256]{1,0:T(8,128)}, u32[]{:S(2)}) %copy-start) | copy-done | bytes 327704
  4.8 0.7 %shard_map.83.table_ref = bf16[8,256,512]{2,1,0:T(8,128)(2,1)S(1)} custom-call(f32[320,256]{1,0:T(8,128)S(1)} %copy-done), custom_call_target="tpu_custom_call" | custom-call | bytes 3145728 | tf_op jit(solution)/shard_map/pallas_call | solution.py:340
  5.5 0.0 copy-start.1
  5.5 0.0 collective-permute-done.other_ref
  5.5 0.9 %shard_map.84 = bf16[16,128,128]{2,1,0:T(8,128)(2,1)S(1)} custom-call(f32[320,256]{1,0:T(8,128)S(1)} %copy-done, bf16[256,256]{1,0:T(8,128)(2,1)S(1)} %collective-permute-done.other_ref, bf16[8,256,512]{2,1,0:T(8,128)(2,1)S(1)} %shard_map.83.table_ref), custom_call_target="tpu_custom_call" | custom-call | flops 536870912 | bytes 1048576 | tf_op jit(solution)/shard_map/pallas_call | solution.py:343
  6.4 19.6 %all_to_all.15.parts_ref = bf16[16,128,128]{2,1,0:T(8,128)(2,1)S(1)} all-to-all(bf16[16,128,128]{2,1,0:T(8,128)(2,1)S(1)} %shard_map.84), channel_id=1, replica_groups={{400,384,464,448,272,256,336,320,144,128,208,192,16,0,80,64},{401,385,4..., dimensions={0} | all-to-all | bytes 1048576 | tf_op jit(solution)/shard_map/all_to_all | solution.py:348
  26.0 0.8 %shard_map.85 = bf16[4,256,128]{2,1,0:T(8,128)(2,1)} custom-call(bf16[16,128,128]{2,1,0:T(8,128)(2,1)S(1)} %all_to_all.15.parts_ref), custom_call_target="tpu_custom_call" | custom-call | bytes 1048576 | tf_op jit(solution)/shard_map/pallas_call | solution.py:349
  26.8 9.8 %all-to-all-start.1 = ((bf16[4,256,128]{2,1,0:T(8,128)(2,1)}), bf16[4,256,128]{2,1,0:T(8,128)(2,1)S(1)}, u32[]{:S(2)}, u32[]{:S(2)}) async-start(bf16[4,256,128]{2,1,0:T(8,128)(2,1)} %shard_map.85), calls=%async_computation.1 | async-start | bytes 524288 | tf_op jit(solution)/shard_map/all_to_all | solution.py:368
  37.3 0.0 copy-done.1
  37.3 1.1 %shard_map.86 = (bf16[6,256,1024]{2,1,0:T(8,128)(2,1)S(1)}, s32[8,128]{1,0:T(8,128)S(1)}) custom-call(s32[1]{0:T(128)S(6)} %copy.9.place_ref, f32[64,256]{1,0:T(8,128)S(1)} %copy-done.1), custom_call_target="tpu_custom_call" | custom-call | bytes 3145728 | tf_op jit(solution)/shard_map/pallas_call | solution.py:359
  38.4 3.7 %all-to-all-done.1.strip_ref = bf16[4,256,128]{2,1,0:T(8,128)(2,1)S(1)} async-done(((bf16[4,256,128]{2,1,0:T(8,128)(2,1)}), bf16[4,256,128]{2,1,0:T(8,128)(2,1)S(1)}, u32[]{:S(2)}, u32[]{:S(2)}) %all-to-all-start.1) | async-done | bytes 262176 | tf_op jit(solution)/shard_map/all_to_all | solution.py:368
  42.1 1.7 %shard_map.87 = bf16[8,128,128]{2,1,0:T(8,128)(2,1)S(1)} custom-call(bf16[4,256,128]{2,1,0:T(8,128)(2,1)S(1)} %all-to-all-done.1.strip_ref, bf16[6,256,1024]{2,1,0:T(8,128)(2,1)S(1)} %get-tuple-element.18.ahead_ref, f32[64,256]{1,0:T(8,128)S(1)} %copy-done.1), custom_call_target="tpu_custom_call" | custom-call | flops 536870912 | bytes 1048576 | tf_op jit(solution)/shard_map/pallas_call | solution.py:369
  43.8 20.0 %all_to_all.16.parts_ref = bf16[8,128,128]{2,1,0:T(8,128)(2,1)S(1)} all-to-all(bf16[8,128,128]{2,1,0:T(8,128)(2,1)S(1)} %shard_map.87), channel_id=1, replica_groups={{12,0,6,2,28,16,22,18},{13,1,7,3,29,17,23,19},{10,14,8,4,26,30,24,20},{..., dimensions={0} | all-to-all | bytes 524288 | tf_op jit(solution)/shard_map/all_to_all | solution.py:377
  63.8 1.0 %shard_map.88 = f32[2,512,128]{2,1,0:T(8,128)} custom-call(s32[8,128]{1,0:T(8,128)S(1)} %get-tuple-element.16.place_ref, bf16[8,128,128]{2,1,0:T(8,128)(2,1)S(1)} %all_to_all.16.parts_ref), custom_call_target="tpu_custom_call" | custom-call | bytes 1048576 | tf_op jit(solution)/shard_map/pallas_call | solution.py:378
Async XLA Ops:
  1.9 3.6 %collective-permute-start = (bf16[256,256]{1,0:T(8,128)(2,1)}, bf16[256,256]{1,0:T(8,128)(2,1)S(1)}, u32[]{:S(2)}, u32[]{:S(2)}) collective-permute-start(bf16[256,256]{1,0:T(8,128)(2,1)} %get-tuple-element.13), channel_id=1, source_target_pairs={{0,32},{32,0},{1,33},{33,1},{2,34},{34,2},{3,35},{35,3},{4,36},{36... | collective-permute-start | bytes 393224 | tf_op jit(solution)/shard_map/ppermute | solution.py:339
  3.9 1.0 %copy-start = (f32[320,256]{1,0:T(8,128)S(1)}, f32[320,256]{1,0:T(8,128)}, u32[]{:S(2)}) copy-start(f32[320,256]{1,0:T(8,128)} %get-tuple-element.12.pack_ref.first_ref) | copy-start | bytes 983044
  5.5 31.8 %copy-start.1 = (f32[64,256]{1,0:T(8,128)S(1)}, f32[64,256]{1,0:T(8,128)}, u32[]{:S(2)}) copy-start(f32[64,256]{1,0:T(8,128)} %get-tuple-element.15.pack_ref) | copy-start | bytes 196612
  26.8 15.3 %all-to-all-start.1 = ((bf16[4,256,128]{2,1,0:T(8,128)(2,1)}), bf16[4,256,128]{2,1,0:T(8,128)(2,1)S(1)}, u32[]{:S(2)}, u32[]{:S(2)}) async-start(bf16[4,256,128]{2,1,0:T(8,128)(2,1)} %shard_map.85), calls=%async_computation.1 | async-start | bytes 524288 | tf_op jit(solution)/shard_map/all_to_all | solution.py:368
